TPU v7x, 32 devices: a whole 2x2x4 slice. The times are simulated.
32 devices in a mesh: gx: 8 (over z, y), gy: 4 (over x, core).
Axes of the slice: x: 2, y: 2, z: 4, core: 2. Of those that a mesh axis runs over, the one named last changes fastest.
Arguments:
- thermal_grid: float32 [32, 64, 128], P('gx', 'gy'), may hold values from -6 to 6
- average_blend_fraction: float32 [32, 64, 128], P('gx', 'gy'), may hold values from 0.05 to 0.95
- normalized_blend_variance: float32 [32, 64, 128], P('gx', 'gy'), may hold values from 0.002 to 0.5
- small_volume_mass: float32 [32, 64, 128], P('gx', 'gy'), may hold values from 0.01 to 0.1
- bare_scalar_decay: float32 [32, 64, 128], P('gx', 'gy'), may hold values from 0.05 to 1
- parent_block: int32 [32, 64, 128], P('gx', 'gy'), may hold values from 0 to 127, as said below
- species_given_block: float32 [128, 16, 128], P(('gx', 'gy')), may hold values from -6 to 6
- block_position: int32 [128], replicated, may hold values from 0 to 127, each once
- face_partners: int32 [128, 6], replicated, may hold values from 0 to 127, as said below
- reaction_increments: int32 [128], replicated, may hold values from 0 to 15, as said below
- chemical_coupling: float32 [16, 16], replicated, may hold values from -1.5 to 1.5
- species_thermal_weight: float32 [16], replicated, may hold values from -1.5 to 1.5
Outputs:
- species_next: float32 [128, 16, 128], P(('gx', 'gy'))
- temperature_next: float32 [32, 64, 128], P('gx', 'gy')
Inputs may be any that keep to these rules, and one draw needn't show every extreme that they name: `parent_block`: each fine cell names the coarse cell under it after a shift of at most 2 fine cells along each dimension; every coarse cell is named. `face_partners`: A cell on the grid's border names itself in place of a missing neighbour; every coarse cell is named. `reaction_increments`: both ends are reached in every draw.
All inputs are finite; a program needn't handle non-finite values.
Results may differ from a plain program's by a relative error of at most 0.0003.
Values sent between devices are 32-bit elements; how exact they have to be, the bound alone decides.
A program may use at most 128 MiB of HBM per device.

v0:
```python
import math

import jax
import jax.numpy as jnp
from jax import lax
from jax.sharding import PartitionSpec as P

ETA = 128
STEPS = 2


coupling = 0.05
mixing_rate = 0.2
react_rate = 0.5
prior_weight = 1.0
prior_flux = 0.5
thermal_diffusion = 0.1
damping_contribution = 0.3


def with_halo(block, sides, width):
    for axis, dim in sides:
        count = lax.axis_size(axis)
        forward = [(i, i + 1) for i in range(count - 1)]
        backward = [(target, source) for source, target in forward]
        low = lax.ppermute(
            lax.slice_in_dim(block, block.shape[dim] - width, None, axis=dim), axis, forward
        )
        high = lax.ppermute(lax.slice_in_dim(block, 0, width, axis=dim), axis, backward)
        block = jnp.concatenate([low, block, high], axis=dim)
    return block


def beta_table(average_blend_fraction, normalized_blend_variance):
    points = (jnp.arange(ETA, dtype=jnp.float32) + 0.5) / ETA
    shape_sum = 1.0 / normalized_blend_variance - 1.0
    alpha = average_blend_fraction * shape_sum
    beta_b = (1.0 - average_blend_fraction) * shape_sum
    logits = (alpha - 1.0)[..., None] * jnp.log(points) + (beta_b - 1.0)[..., None] * jnp.log(
        1.0 - points
    )
    return jax.nn.softmax(logits, axis=-1)


def lap_mixture(field):
    bordered_grid = jnp.concatenate([field[..., :1], field, field[..., -1:]], axis=-1)
    return bordered_grid[..., 2:] - 2.0 * field + bordered_grid[..., :-2]


def coarse_advance(fluid_condition, nearby, scalar_decay_speed, counts, chemical_coupling, turns):
    fluid_condition = fluid_condition + coupling * jnp.sum(
        nearby - fluid_condition[:, None], axis=1
    )
    fraction = 1.0 / counts.astype(jnp.float32)

    def substep(index, current):
        source = jnp.einsum(
            "st,ctk->csk", chemical_coupling, jnp.tanh(current), precision=lax.Precision.HIGHEST
        )
        update = fraction[:, None, None] * (
            mixing_rate * scalar_decay_speed[:, None, :] * lap_mixture(current)
            + react_rate * source
        )
        return jnp.where((index < counts)[:, None, None], current + update, current)

    return lax.fori_loop(0, turns, substep, fluid_condition)


def cell_blocks(cells):
    width = math.gcd(cells, 512)
    return (cells // width, width)


def small_volume_accumulations(
    tabulated_values,
    small_volume_mass,
    bare_scalar_decay,
    thermal_grid,
    parent_block,
    block_numbers,
):
    points = tabulated_values.shape[-1]
    cells = parent_block.size
    nblocks, width = cell_blocks(cells)
    flat_table = tabulated_values.reshape(nblocks, width, points)
    flat_mass = small_volume_mass.reshape(nblocks, width, 1)
    flat_speed = (bare_scalar_decay * (1.0 + 0.5 * jnp.tanh(thermal_grid))).reshape(
        nblocks, width, 1
    )
    flat_parent = parent_block.reshape(nblocks, width)
    labels = jnp.arange(block_numbers, dtype=jnp.int32)

    def attach_block(total, pieces):
        table_piece, mass_piece, speed_piece, parent_piece = pieces
        weighted = mass_piece * table_piece
        values = jnp.concatenate([weighted, weighted * speed_piece], axis=-1)
        selector = (parent_piece[:, None] == labels[None, :]).astype(jnp.float32)
        added = lax.dot_general(
            selector,
            values,
            (((0,), (0,)), ((), ())),
            precision=lax.Precision.HIGHEST,
            preferred_element_type=jnp.float32,
        )
        return (total + added, None)

    start_total = jnp.zeros((block_numbers, 2 * points), jnp.float32)
    total, unused = lax.scan(
        attach_block, start_total, (flat_table, flat_mass, flat_speed, flat_parent)
    )
    return total.reshape(block_numbers, 2, points)


def coarse_to_fine(tabulated_values, blend_block_number, parent_block):
    points = tabulated_values.shape[-1]
    block_numbers = blend_block_number.shape[0]
    cells = parent_block.size
    nblocks, width = cell_blocks(cells)
    flat_table = tabulated_values.reshape(nblocks, width, points)
    flat_parent = parent_block.reshape(nblocks, width)
    labels = jnp.arange(block_numbers, dtype=jnp.int32)

    def one_block(pieces):
        table_piece, parent_piece = pieces
        selector = (parent_piece[:, None] == labels[None, :]).astype(jnp.float32)
        picked = jnp.dot(
            selector,
            blend_block_number,
            precision=lax.Precision.HIGHEST,
            preferred_element_type=jnp.float32,
        )
        return jnp.sum(table_piece * picked, axis=-1)

    return lax.map(one_block, (flat_table, flat_parent)).reshape(parent_block.shape)


def advance_small_fluid(thermal_grid, tabulated_values, blend_block_number, parent_block):
    bordered_grid = with_halo(thermal_grid, (("gx", 0), ("gy", 1)), 1)
    small_grid_thermal = coarse_to_fine(tabulated_values, blend_block_number, parent_block)
    bordered_grid = jnp.pad(bordered_grid, ((0, 0), (0, 0), (1, 1)))
    nearby_blocks = bordered_grid[2:, 1:-1, 1:-1] + bordered_grid[:-2, 1:-1, 1:-1]
    nearby_blocks = nearby_blocks + bordered_grid[1:-1, 2:, 1:-1] + bordered_grid[1:-1, :-2, 1:-1]
    nearby_blocks = nearby_blocks + bordered_grid[1:-1, 1:-1, 2:] + bordered_grid[1:-1, 1:-1, :-2]
    return (
        thermal_grid
        + thermal_diffusion * (nearby_blocks - 6.0 * thermal_grid)
        + damping_contribution * (small_grid_thermal - thermal_grid)
    )


def shards(
    thermal_grid,
    average_blend_fraction,
    normalized_blend_variance,
    small_volume_mass,
    bare_scalar_decay,
    parent_block,
    species_given_block,
    block_position,
    face_partners,
    reaction_increments,
    chemical_coupling,
    species_thermal_weight,
):
    block_numbers = block_position.shape[0]
    owned = species_given_block.shape[0]
    device_index = lax.axis_index("gx") * lax.axis_size("gy") + lax.axis_index("gy")
    position_block_map = jnp.argsort(block_position)
    near_slot = block_position[face_partners[position_block_map]]
    counts = reaction_increments[position_block_map] + 1
    tabulated_values = beta_table(average_blend_fraction, normalized_blend_variance)
    state_all = lax.all_gather(species_given_block, ("gx", "gy"), axis=0, tiled=True)
    for turn in range(STEPS):
        local_aggregates = small_volume_accumulations(
            tabulated_values,
            small_volume_mass,
            bare_scalar_decay,
            thermal_grid,
            parent_block,
            block_numbers,
        )
        totals = lax.psum(local_aggregates[position_block_map], ("gx", "gy"))
        cchi_all = (totals[:, 1] + prior_flux) / (totals[:, 0] + prior_weight)
        state_all = coarse_advance(
            state_all, state_all[near_slot], cchi_all, counts, chemical_coupling, jnp.max(counts)
        )
        blend_position = jnp.einsum(
            "s,csk->ck", species_thermal_weight, state_all, precision=lax.Precision.HIGHEST
        )
        thermal_grid = advance_small_fluid(
            thermal_grid, tabulated_values, blend_position[block_position], parent_block
        )
    local_condition = lax.dynamic_slice_in_dim(state_all, device_index * owned, owned, 0)
    return (local_condition, thermal_grid)


def solution(mesh):
    placed = (
        P("gx", "gy", None),
        P("gx", "gy", None),
        P("gx", "gy", None),
        P("gx", "gy", None),
        P("gx", "gy", None),
        P("gx", "gy", None),
        P(("gx", "gy"), None, None),
        P(),
        P(),
        P(),
        P(),
        P(),
    )
    return jax.shard_map(
        shards,
        mesh=mesh,
        in_specs=placed,
        out_specs=(P(("gx", "gy"), None, None), P("gx", "gy", None)),
        check_vma=False,
    )
```

profile of v0, /device:TPU:0, one launch (start us, length us, event | category | flops | bytes accessed | tf_op | source)
XLA Modules:
  0.0 596.9 jit_solution(453682543400922179)
XLA Ops:
  8.0 4.9 collective-permute-start.1
  13.7 3.8 fusion.38
  17.5 5.2 exponential_reduce_fusion
  22.7 3.2 sort.17
  25.9 6.3 %exponential_divide_fusion = f32[16,512,128]{2,1,0:T(8,128)} fusion(f32[16,512]{1,0:T(8,128)S(1)} %div.46, f32[16,512]{1,0:T(8,128)S(1)} %sub.77, f32[128]{0:T(128)S(1)} %get-tuple-element.484, f32[16,512]{1,0:T(8,128)S(1)} %mul.211, f32[128]{0:T(128)S(1)} %get-tuple-element.485, f32[16,512]{1,0:T(8,128)S(1)} %mul.206), kind=kLoop, calls=%fused_computation.78 | loop fusion | flops 5242880 | bytes 4326400 | tf_op jit(solution)/shard_map/div | solution.py:42
  32.3 39.1 %while.68 = (s32[]{:T(128)}, f32[128,256]{1,0:T(8,128)S(1)}, s32[16,512]{1,0:T(8,128)S(1)}, f32[16,512,1]{1,2,0:T(1,128)}, f32[16,512,128]{2,1,0:T(8,128)}, /*index=5*/f32[16,512,1]{1,2,0:T(1,128)S(1)}, s32[]{:T(128)}, s32[]{:T(128)}) while((s32[]{:T(128)}, f32[128,256]{1,0:T(8,128)S(1)}, s32[16,512]{1,0:T(8,128)S(1)}, ...), condition=%wide.region_6.7_spmd.clone, body=%wide.region_5.6_spmd.clone.sunk | while | flops 201719808 | bytes 1591411 | solution.py:108
  71.5 1.4 gather_fusion.4
  75.3 4.8 gather_fusion.1
  83.6 3.0 collective-permute-start.3
  86.7 5.4 copy.31
  92.2 103.6 %all-reduce.5.cloned.1.call-done = f32[128,2,128]{2,1,0:T(2,128)} async-done(((f32[128,2,128]{2,1,0:T(2,128)}), f32[128,2,128]{2,1,0:T(2,128)}) %all-reduce.5.cloned.1.call-update) | async-done | bytes 131088 | tf_op jit(solution)/shard_map/psum | solution.py:182
  196.9 54.5 %all-gather.2.cloned.1.call-done = f32[128,16,128]{2,1,0:T(8,128)} async-done(((f32[4,16,128]{2,1,0:T(8,128)}), f32[128,16,128]{2,1,0:T(8,128)}) %all-gather.2.cloned.1.call-update) | async-done | bytes 1048592 | tf_op jit(solution)/shard_map/all_gather | solution.py:172
  251.4 5.1 gather_fusion.2
  256.6 4.3 subtract_reduce_fusion.1
  261.0 47.8 %while.64 = (s32[]{:T(128)}, f32[128,16,128]{2,1,0:T(8,128)S(1)}, s32[]{:T(128)}, s32[128]{0:T(128)S(1)}, f32[128]{0:T(128)S(1)}, /*index=5*/f32[128,128]{1,0:T(8,128)S(1)}, f32[16,16]{1,0:T(8,128)S(1)}, s32[]{:T(128)}) while((s32[]{:T(128)}, f32[128,16,128]{2,1,0:T(8,128)S(1)}, s32[]{:T(128)}, s32[128]{0:T(128)S(1)}, f32[128]{0:T(128)S(1)}, ...), condition=%wide.region_9.10_spmd, body=%wide.region_8.9_spmd.sunk | while | flops 53231744 | bytes 4442465 | solution.py:66
  262.0 1.9 add_select_fusion.4
  265.0 1.9 add_select_fusion.4
  267.9 1.9 add_select_fusion.4
  270.9 1.9 add_select_fusion.4
  273.8 1.9 add_select_fusion.4
  276.8 1.9 add_select_fusion.4
  279.7 1.9 add_select_fusion.4
  282.7 1.9 add_select_fusion.4
  285.6 1.9 add_select_fusion.4
  288.6 1.9 add_select_fusion.4
  291.5 1.9 add_select_fusion.4
  294.5 1.9 add_select_fusion.4
  297.4 1.9 add_select_fusion.4
  300.4 1.9 add_select_fusion.4
  303.4 1.9 add_select_fusion.4
  306.3 1.9 add_select_fusion.4
  308.8 4.0 gather_fusion.5
  314.1 23.6 %while.66 = (s32[]{:T(128)}, f32[16,512]{1,0:T(8,128)S(1)}, f32[16,512,128]{1,2,0:T(8,128)}, s32[16,512]{1,0:T(8,128)S(1)}, f32[128,128]{1,0:T(8,128)S(1)}, /*index=5*/s32[]{:T(128)}, s32[]{:T(128)}) while((s32[]{:T(128)}, f32[16,512]{1,0:T(8,128)S(1)}, f32[16,512,128]{1,2,0:T(8,128)}, s32[16,512]{1,0:T(8,128)S(1)}, ...), condition=%wide.region_13.14_spmd.clone, body=%wide.region_11.13_spmd.clone.sunk | while | flops 100859392 | bytes 340065 | solution.py:134
  321.5 1.4 fusion.91
  324.4 1.4 fusion.91
  330.3 1.4 fusion.91
  336.2 1.4 fusion.91
  337.8 39.1 %while.69 = (s32[]{:T(128)}, f32[128,256]{1,0:T(8,128)S(1)}, s32[16,512]{1,0:T(8,128)S(1)}, f32[16,512,1]{1,2,0:T(1,128)}, f32[16,512,128]{2,1,0:T(8,128)}, /*index=5*/f32[16,512,1]{1,2,0:T(1,128)S(1)}, s32[]{:T(128)}, s32[]{:T(128)}) while((s32[]{:T(128)}, f32[128,256]{1,0:T(8,128)S(1)}, s32[16,512]{1,0:T(8,128)S(1)}, ...), condition=%wide.region_15.16_spmd.clone, body=%wide.region_14.15_spmd.clone.sunk | while | flops 201719808 | bytes 1591411 | solution.py:108
  378.2 4.7 collective-permute-start.5
  382.9 4.3 subtract_reduce_fusion
  388.5 3.0 collective-permute-start.7
  391.8 1.4 gather_fusion.7
  393.3 121.8 %all-reduce.7.cloned.1.call-done = f32[128,2,128]{2,1,0:T(2,128)} async-done(((f32[128,2,128]{2,1,0:T(2,128)}), f32[128,2,128]{2,1,0:T(2,128)}) %all-reduce.7.cloned.1.call-update) | async-done | bytes 131088 | tf_op jit(solution)/shard_map/psum | solution.py:182
  516.3 47.8 %while.65 = (s32[]{:T(128)}, f32[128,16,128]{2,1,0:T(8,128)S(1)}, s32[]{:T(128)}, s32[128]{0:T(128)S(1)}, f32[128]{0:T(128)S(1)}, /*index=5*/f32[128,128]{1,0:T(8,128)S(1)}, f32[16,16]{1,0:T(8,128)S(1)}, s32[]{:T(128)}) while((s32[]{:T(128)}, f32[128,16,128]{2,1,0:T(8,128)S(1)}, s32[]{:T(128)}, s32[128]{0:T(128)S(1)}, f32[128]{0:T(128)S(1)}, ...), condition=%wide.region_18.19_spmd, body=%wide.region_17.18_spmd.sunk | while | flops 53231744 | bytes 4442465 | solution.py:66
  517.3 1.9 add_select_fusion.5
  520.2 1.9 add_select_fusion.5
  523.2 1.9 add_select_fusion.5
  526.1 1.9 add_select_fusion.5
  529.1 1.9 add_select_fusion.5
  532.0 1.9 add_select_fusion.5
  535.0 1.9 add_select_fusion.5
  538.0 1.9 add_select_fusion.5
  540.9 1.9 add_select_fusion.5
  543.9 1.9 add_select_fusion.5
  546.8 1.9 add_select_fusion.5
  549.8 1.9 add_select_fusion.5
  552.7 1.9 add_select_fusion.5
  555.7 1.9 add_select_fusion.5
  558.6 1.9 add_select_fusion.5
  561.6 1.9 add_select_fusion.5
  566.0 23.6 %while.67 = (s32[]{:T(128)}, f32[16,512]{1,0:T(8,128)S(1)}, f32[16,512,128]{1,2,0:T(8,128)}, s32[16,512]{1,0:T(8,128)S(1)}, f32[128,128]{1,0:T(8,128)S(1)}, /*index=5*/s32[]{:T(128)}, s32[]{:T(128)}) while((s32[]{:T(128)}, f32[16,512]{1,0:T(8,128)S(1)}, f32[16,512,128]{1,2,0:T(8,128)}, s32[16,512]{1,0:T(8,128)S(1)}, ...), condition=%wide.region_21.22_spmd.clone, body=%wide.region_19.21_spmd.clone.sunk | while | flops 100859392 | bytes 340065 | solution.py:134
  573.4 1.4 fusion.93
  576.4 1.4 fusion.93
  579.3 1.4 fusion.93
  (432 shorter events, 143.9 us)
Async XLA Ops:
  7.2 305.6 %copy-start = (f32[16]{0:T(128)S(1)}, f32[16]{0:T(128)}, u32[]{:S(2)}) copy-start(f32[16]{0:T(128)} %param.35) | copy-start | bytes 196
  7.2 25.1 %copy-start.5 = (f32[4,16,128]{2,1,0:T(8,128)S(1)}, f32[4,16,128]{2,1,0:T(8,128)}, u32[]{:S(2)}) copy-start(f32[4,16,128]{2,1,0:T(8,128)} %param.24) | copy-start | bytes 98308
  7.2 25.0 %copy-start.7 = (s32[4,16,128]{2,1,0:T(8,128)S(1)}, s32[4,16,128]{2,1,0:T(8,128)}, u32[]{:S(2)}) copy-start(s32[4,16,128]{2,1,0:T(8,128)} %param.29) | copy-start | bytes 98308
  7.2 25.1 %copy-start.6 = (f32[4,16,128]{2,1,0:T(8,128)S(1)}, f32[4,16,128]{2,1,0:T(8,128)}, u32[]{:S(2)}) copy-start(f32[4,16,128]{2,1,0:T(8,128)} %param.28) | copy-start | bytes 98308
  7.2 188.6 %all-reduce.5.cloned.1.call-start = ((), (), s32[]{:S(2)}) async-start(), calls=%async_computation.1 | async-start | bytes 262144 | tf_op jit(solution)/shard_map/psum | solution.py:182
  8.0 24.3 %collective-permute-start.1 = (f32[1,16,128]{2,1,0:T(8,128)S(1)}, f32[1,16,128]{2,1,0:T(8,128)S(1)}, u32[]{:S(2)}, u32[]{:S(2)}) collective-permute-start(f32[1,16,128]{2,1,0:T(8,128)S(1)} %get-tuple-element.477), channel_id=1, source_target_pairs={{0,4},{4,8},{8,12},{12,16},{16,20},{20,24},{24,28},{1,5},{5,9},{9,... | collective-permute-start | bytes 24584 | tf_op jit(solution)/shard_map/ppermute | solution.py:26
  32.3 42.0 %copy-start.8 = (s32[128,6]{0,1:T(8,128)S(1)}, s32[128,6]{0,1:T(8,128)}, u32[]{:S(2)}) copy-start(s32[128,6]{0,1:T(8,128)} %param.32) | copy-start | bytes 9220
  32.3 42.9 %copy-start.1 = (s32[128]{0:T(128)S(1)}, s32[128]{0:T(128)}, u32[]{:S(2)}) copy-start(s32[128]{0:T(128)} %param.31) | copy-start | bytes 1540
  72.9 178.5 %all-gather.2.cloned.1.call-start = ((), (), s32[]{:S(2)}) async-start(), calls=%async_computation | async-start | bytes 1081344 | tf_op jit(solution)/shard_map/all_gather | solution.py:172
  73.0 9.3 %collective-permute-start = (f32[1,16,128]{2,1,0:T(8,128)S(1)}, f32[1,16,128]{2,1,0:T(8,128)S(1)}, u32[]{:S(2)}, u32[]{:S(2)}) collective-permute-start(f32[1,16,128]{2,1,0:T(8,128)S(1)} %get-tuple-element.476), channel_id=1, source_target_pairs={{4,0},{8,4},{12,8},{16,12},{20,16},{24,20},{28,24},{5,1},{9,5},{13... | collective-permute-start | bytes 24584 | tf_op jit(solution)/shard_map/ppermute | solution.py:29
  74.3 440.9 %all-reduce.7.cloned.1.call-start = ((), (), s32[]{:S(2)}) async-start(), calls=%async_computation.2 | async-start | bytes 262144 | tf_op jit(solution)/shard_map/psum | solution.py:182
  75.3 4.9 copy-start.2
  82.3 9.7 %collective-permute-start.2 = (f32[6,1,128]{2,1,0:T(1,128)S(1)}, f32[6,1,128]{2,1,0:T(1,128)S(1)}, u32[]{:S(2)}, u32[]{:S(2)}) collective-permute-start(f32[6,1,128]{2,1,0:T(1,128)S(1)} %get-tuple-element.473), channel_id=1, source_target_pairs={{1,0},{2,1},{3,2},{5,4},{6,5},{7,6},{9,8},{10,9},{11,10},{13,12},{... | collective-permute-start | bytes 9224 | tf_op jit(solution)/shard_map/ppermute | solution.py:29
  83.6 8.4 %collective-permute-start.3 = (f32[6,1,128]{2,1,0:T(1,128)S(1)}, f32[6,1,128]{2,1,0:T(1,128)S(1)}, u32[]{:S(2)}, u32[]{:S(2)}) collective-permute-start(f32[6,1,128]{2,1,0:T(1,128)S(1)} %get-tuple-element.472), channel_id=1, source_target_pairs={{0,1},{1,2},{2,3},{4,5},{5,6},{6,7},{8,9},{9,10},{10,11},{12,13},{... | collective-permute-start | bytes 9224 | tf_op jit(solution)/shard_map/ppermute | solution.py:26
  251.4 5.2 copy-start.3
  256.6 4.4 copy-start.4
  376.9 10.3 %collective-permute-start.4 = (f32[1,16,128]{2,1,0:T(8,128)S(1)}, f32[1,16,128]{2,1,0:T(8,128)S(1)}, u32[]{:S(2)}, u32[]{:S(2)}) collective-permute-start(f32[1,16,128]{2,1,0:T(8,128)S(1)} %get-tuple-element.475), channel_id=1, source_target_pairs={{4,0},{8,4},{12,8},{16,12},{20,16},{24,20},{28,24},{5,1},{9,5},{13... | collective-permute-start | bytes 24584 | tf_op jit(solution)/shard_map/ppermute | solution.py:29
  378.2 9.0 %collective-permute-start.5 = (f32[1,16,128]{2,1,0:T(8,128)S(1)}, f32[1,16,128]{2,1,0:T(8,128)S(1)}, u32[]{:S(2)}, u32[]{:S(2)}) collective-permute-start(f32[1,16,128]{2,1,0:T(8,128)S(1)} %get-tuple-element.474), channel_id=1, source_target_pairs={{0,4},{4,8},{8,12},{12,16},{16,20},{20,24},{24,28},{1,5},{5,9},{9,... | collective-permute-start | bytes 24584 | tf_op jit(solution)/shard_map/ppermute | solution.py:26
  387.2 6.0 collective-permute-start.6
  388.5 4.7 collective-permute-start.7
Sparse Core Ops, SparseCore 0:
  73.0 122.7 all-reduce.4
  198.7 52.6 all-gather.1
  393.3 121.8 all-reduce.6
where the time goes:
time: 601 us; the launch traced here: 597 us
  waiting for transfers between devices  280 us (47%)
  matrix products  124 us (21%)
  other arithmetic  69.2 us (12%)
  local copies, waits for them, and re-layouts  65.2 us (11%)
  loops' own time  22.8 us (4%)
  starting transfers between devices  20.9 us (3%)
  between operations  14.3 us (2%)
    psum x2, waiting for transfers between devices, shards(): totals = lax.psum(local_aggregates[position_block_map], ('gx', 'gy'))  225 us
    dot_general x32, matrix products, substep(): jnp.einsum('st,ctk->csk', chemical_coupling, jnp.tanh(current), precision...  61.6 us
    all_gather x1, waiting for transfers between devices, shards(): lax.all_gather(species_given_block, ('gx', 'gy'), axis=0, tiled=True)  54.5 us
    dot_general x32, matrix products, one_block(): jnp.dot(selector, blend_block_number, precision=lax.Precision.HIGHEST, pr...  43.7 us
    mul x32, other arithmetic, attach_block(): values = jnp.concatenate([weighted, weighted * speed_piece], axis=-1)  36.6 us
    dynamic_slice x96, local copies, waits for them, and re-layouts, small_volume_accumulations(): lax.scan(attach_block, start_total, (flat_table, flat_mass, flat_speed, f...  22.7 us
    another operation x2, loops' own time, coarse_advance(): return lax.fori_loop(0, turns, substep, fluid_condition)  20.3 us
    dot_general x32, matrix products, attach_block(): lax.dot_general(selector, values, (((0,), (0,)), ((), ())), precision=lax...  17.7 us
  transfers between devices with their start and end apart: 11, of which 3 were waited for; matrix products, arithmetic and copies ran while one was open for 7% of the time, Pallas kernels for 0%

commit v1 on v0

v1 whole, which is shorter than its diff:
```python
import functools

import jax
import jax.numpy as jnp
from jax import lax
from jax.experimental import pallas as pl
from jax.experimental.pallas import tpu as pltpu
from jax.sharding import PartitionSpec as P

ETA = 128
SPEC = 16
SUBMAX = 16
STEPS = 2
ROWS = 4
OWNED = 4

coupling = 0.05
mixing_rate = 0.2
react_rate = 0.5
prior_weight = 1.0
prior_flux = 0.5
thermal_diffusion = 0.1
damping_contribution = 0.3

MESH = pl.DeviceIdType.MESH
HIGHEST = lax.Precision.HIGHEST
NT = (((1,), (1,)), ((), ()))
f32, bf16, i32 = jnp.float32, jnp.bfloat16, jnp.int32


def kernel(
    gxn, gyn, xs, ys,
    thermal, mean, variance, mass, decay, parent, state0, position_row, chem, weight,
    position, partners, increments,
    species_out, thermal_out,
    ids, log_a, log_b, shape_a, shape_b, chi, grid, fine, table, table16, total,
    sent, got, theta, state, face_x, face_y, own_y,
    sums_send, sums_recv, theta_send, theta_recv, state_send, state_recv, halo_send, halo_recv,
):
    ndev = gxn * gyn
    blocks = ndev * OWNED
    rows = xs * ys
    turns = rows // ROWS
    pairs = gyn // 2
    gx, gy = lax.axis_index("gx"), lax.axis_index("gy")
    me = gx * gyn + gy
    core, pair = lax.rem(gy, 2), gy // 2

    def place(device):
        device = lax.rem(device + ndev, ndev)
        return (device // gyn, lax.rem(device, gyn))

    barrier = pltpu.get_barrier_semaphore()

    @pl.loop(1, ndev)
    def _(j):
        pl.semaphore_signal(barrier, inc=1, device_id=place(me + j), device_id_type=MESH)

    row = lax.broadcasted_iota(i32, (ndev * 8, blocks), 0)
    device = me - (row >> 3)
    slot = jnp.where(device < 0, device + ndev, device) * OWNED + (row & 3)
    hit = position_row[...] == slot
    cell = lax.broadcasted_iota(i32, (ndev * 8, blocks), 1).astype(f32)
    named = jnp.sum(jnp.where(hit, cell, 0.0), axis=1, keepdims=True).astype(i32)
    ids[...] = jnp.broadcast_to(named, (ndev * 8, 128)).reshape(ndev, 8, 128)

    points = (lax.broadcasted_iota(i32, (ETA, 128), 0).astype(f32) + 0.5) / ETA
    log_a[...] = jnp.log(points)
    log_b[...] = jnp.log(1.0 - points)
    shape_sum = 1.0 / variance[...] - 1.0
    shape_a[...] = mean[...] * shape_sum - 1.0
    shape_b[...] = (1.0 - mean[...]) * shape_sum - 1.0
    grid[...] = thermal[...]

    spread = (
        (lax.broadcasted_iota(i32, (OWNED * SPEC, SPEC), 0) & (SPEC - 1))
        == lax.broadcasted_iota(i32, (OWNED * SPEC, SPEC), 1)
    ).astype(f32)
    wide = jnp.dot(spread, chem[...], precision=HIGHEST, preferred_element_type=f32)
    wide = lax.dot_general(wide, spread, NT, precision=HIGHEST, preferred_element_type=f32)
    same = (lax.broadcasted_iota(i32, wide.shape, 0) >> 4) == (
        lax.broadcasted_iota(i32, wide.shape, 1) >> 4
    )
    wide = jnp.where(same, wide, 0.0)
    wide_high = wide.astype(bf16)
    wide_low = (wide - wide_high.astype(f32)).astype(bf16)
    chem_all = jnp.concatenate([wide_high, wide_low], axis=0)

    weights = lax.dot_general(
        jnp.broadcast_to(weight[...], (8, SPEC)), spread, NT,
        precision=HIGHEST, preferred_element_type=f32,
    )
    mine = (lax.broadcasted_iota(i32, weights.shape, 0) & 3) == (
        lax.broadcasted_iota(i32, weights.shape, 1) >> 4
    )
    weights = jnp.where(mine, weights, 0.0)

    pl.semaphore_wait(barrier, ndev - 1)

    pending = []

    def along_gx(turn, j):
        def block(x):
            return state.at[turn, core, pair, x]

        there = (lax.rem(gx + j, gxn), gy)
        here = block(gx)
        come = block(lax.rem(gx - j + gxn, gxn))
        sems = (state_send.at[turn, j - 1], state_recv.at[turn, j - 1])
        return (
            pltpu.make_async_remote_copy(here, here, *sems, there, MESH),
            pltpu.make_async_remote_copy(come, come, *sems, there, MESH),
        )

    def along_pair(turn, j):
        other = lax.rem(pair + j, pairs)
        there = (gx, other * 2 + core)
        here = state.at[turn, core, pair]
        come = state.at[turn, core, lax.rem(pair - j + pairs, pairs)]
        sems = (state_send.at[turn, gxn - 2 + j], state_recv.at[turn, gxn - 2 + j])
        return (
            pltpu.make_async_remote_copy(here, here, *sems, there, MESH),
            pltpu.make_async_remote_copy(come, come, *sems, there, MESH),
        )

    def across(turn):
        there = (gx, pair * 2 + 1 - core)
        here = state.at[turn, core]
        come = state.at[turn, 1 - core]
        last = gxn + pairs - 2
        sems = (state_send.at[turn, last], state_recv.at[turn, last])
        return (
            pltpu.make_async_remote_copy(here, here, *sems, there, MESH),
            pltpu.make_async_remote_copy(come, come, *sems, there, MESH),
        )

    def launch(copies):
        for out, _ in copies:
            out.start()
            pending.append(out)

    def arrive(copies):
        for _, come in copies:
            come.wait_recv()

    def leg(turn, which):
        if which == 0:
            return [along_gx(turn, j) for j in range(1, gxn)]
        if which == 1:
            return [along_pair(turn, j) for j in range(1, pairs)]
        return [across(turn)]

    def halo(turn):
        low = (lax.rem(gx - 1 + gxn, gxn), gy)
        high = (lax.rem(gx + 1, gxn), gy)
        left = (gx, lax.rem(gy - 1 + gyn, gyn))
        right = (gx, lax.rem(gy + 1, gyn))
        source = grid if turn else thermal
        first = source.at[pl.ds(0, ys)]
        last = source.at[pl.ds((xs - 1) * ys, ys)]
        ends = [
            (last, face_x.at[turn, 0], high),
            (first, face_x.at[turn, 1], low),
            (own_y.at[turn], face_y.at[turn, 0], right),
            (own_y.at[turn], face_y.at[turn, 1], left),
        ]
        copies = [
            pltpu.make_async_remote_copy(
                s, d, halo_send.at[turn, n], halo_recv.at[turn, n], there, MESH
            )
            for n, (s, d, there) in enumerate(ends)
        ]
        return [(c, c) for c in copies]

    def send_halo(turn):
        now = grid[...]
        own_y[turn] = jnp.concatenate(
            [now[x * ys : x * ys + 1] for x in range(xs)]
            + [now[x * ys + ys - 1 : (x + 1) * ys] for x in range(xs)],
            axis=0,
        )
        launch(halo(turn))

    def exchange(source, target, turn, sign, send, recv):
        @pl.loop(1, ndev)
        def _(j):
            pltpu.make_async_remote_copy(
                source(j), target.at[turn, j], send.at[turn], recv.at[turn],
                place(me + sign * j), MESH,
            ).start()

        rest = target.at[turn, pl.ds(1, ndev - 1)]
        whole = pltpu.make_async_remote_copy(
            rest, rest, send.at[turn], recv.at[turn], place(me + 1), MESH
        )
        pending.append(whole)
        whole.wait_recv()

    half_row = lax.broadcasted_iota(i32, (8, 128), 0) < 4

    def gather_row(r):
        here = mass[pl.ds(r, 1), :]
        both = jnp.where(half_row, here, here * chi[pl.ds(r, 1), :])
        chosen = jnp.where(parent[pl.ds(r, 1), :][None] == ids[...], both[None], 0.0)
        return chosen.reshape(ndev * 8, 128).astype(bf16)

    def add_up(i, chosen, values):
        total[...] += lax.dot_general(
            jnp.concatenate(chosen, axis=1), values, NT, preferred_element_type=f32
        )

    def first_turn(i, cells):
        chosen = []
        for n in range(ROWS):
            r = i * ROWS + n
            logits = shape_a[pl.ds(r, 1), :] * log_a[...] + shape_b[pl.ds(r, 1), :] * log_b[...]
            raised = jnp.exp(logits - jnp.max(logits, axis=0, keepdims=True))
            part = raised * (1.0 / jnp.sum(raised, axis=0, keepdims=True))
            table[i, :, n * 128 : (n + 1) * 128] = part
            table16[i, :, n * 128 : (n + 1) * 128] = part.astype(bf16)
            chosen.append(gather_row(r))
        add_up(i, chosen, table16[i])
        each = blocks // turns
        for n in range(each):
            c = i * each + n
            at = position[c]
            cells = tuple(
                jnp.where(at == me * OWNED + q, c, cells[q]) for q in range(OWNED)
            )
        return cells

    def second_turn(i, carry):
        add_up(i, [gather_row(i * ROWS + n) for n in range(ROWS)], table16[i])
        return carry

    def reduce_sums(turn):
        sent[turn] = total[...].reshape(ndev, 8, 128)
        exchange(lambda j: sent.at[turn, j], got, turn, -1, sums_send, sums_recv)
        return sent[turn, 0] + jnp.sum(got[turn, pl.ds(1, ndev - 1)], axis=0)

    def spread_rows(pieces):
        return jnp.concatenate(
            [jnp.broadcast_to(p, (SPEC, 128)) for p in pieces], axis=0
        )

    lane = lax.broadcasted_iota(i32, (OWNED * SPEC, 128), 1)

    def advance(turn, sums, cells):
        cchi = (sums[4:8] + prior_flux) / (sums[0:4] + prior_weight)
        cchi = spread_rows([cchi[q : q + 1] for q in range(OWNED)])
        counts = jnp.concatenate(
            [jnp.full((SPEC, 128), increments[cells[q]] + 1, i32) for q in range(OWNED)], axis=0
        )
        fraction = 1.0 / counts.astype(f32)
        mixed = fraction * mixing_rate * cchi
        reacted = fraction * react_rate
        parts = []
        for q in range(OWNED):
            around = None
            for j in range(6):
                near = position[partners[cells[q] * 6 + j]]
                d = near >> 2
                y = lax.rem(d, gyn)
                there = state[
                    turn, lax.rem(y, 2), y // 2, d // gyn, pl.ds((near & 3) * SPEC, SPEC), :
                ]
                around = there if around is None else around + there
            parts.append(around)
        around = jnp.concatenate(parts, axis=0)
        now = state0[...] if turn == 0 else species_out[...]
        now = now + coupling * (around - 6.0 * now)

        def substep(index, current):
            bent = jnp.tanh(current)
            high = bent.astype(bf16)
            low = (bent - high.astype(f32)).astype(bf16)
            source = jnp.dot(
                chem_all, jnp.concatenate([high, low], axis=1), preferred_element_type=f32
            )
            n = OWNED * SPEC
            source = source[:n, :128] + (source[:n, 128:] + source[n:, :128])
            left = jnp.where(lane == 0, current, pltpu.roll(current, 1, 1))
            right = jnp.where(lane == 127, current, pltpu.roll(current, 127, 1))
            update = mixed * (right - 2.0 * current + left) + reacted * source
            return jnp.where(index < counts, current + update, current)

        now = lax.fori_loop(0, SUBMAX, substep, now)
        species_out[...] = now
        theta[turn, 0] = jnp.dot(weights, now, precision=HIGHEST, preferred_element_type=f32)
        return now

    def refine(turn):
        exchange(lambda j: theta.at[turn, 0], theta, turn, 1, theta_send, theta_recv)
        whole = theta[turn]
        high = whole.astype(bf16).astype(f32)
        halves = jnp.where(half_row[None], high, whole - high).reshape(ndev * 8, 128)
        halves = halves.T.astype(bf16)

        def body(i, carry):
            picks = [
                jnp.where(parent[pl.ds(i * ROWS + n, 1), :][None] == ids[...], 1.0, 0.0)
                .reshape(ndev * 8, 128)
                .astype(bf16)
                for n in range(ROWS)
            ]
            picked = jnp.dot(
                halves, jnp.concatenate(picks, axis=1), preferred_element_type=f32
            )
            value = jnp.sum(table[i] * picked, axis=0, keepdims=True)
            for n in range(ROWS):
                fine[pl.ds(i * ROWS + n, 1), :] = value[:, n * 128 : (n + 1) * 128]
            return carry

        lax.fori_loop(0, turns, body, 0)

    def diffuse(turn):
        arrive(halo(turn))
        now = grid[...]
        zero = jnp.zeros((ys, 128), f32)
        low_x = jnp.where(gx == 0, zero, face_x[turn, 0])
        high_x = jnp.where(gx == gxn - 1, zero, face_x[turn, 1])
        around = jnp.concatenate([now[ys:], high_x], axis=0)
        around = around + jnp.concatenate([low_x, now[:-ys]], axis=0)
        low_y = jnp.where(gy == 0, 0.0, face_y[turn, 0])
        high_y = jnp.where(gy == gyn - 1, 0.0, face_y[turn, 1])
        low_y = jnp.concatenate(
            [jnp.broadcast_to(low_y[xs + x : xs + x + 1], (ys, 128)) for x in range(xs)], axis=0
        )
        high_y = jnp.concatenate(
            [jnp.broadcast_to(high_y[x : x + 1], (ys, 128)) for x in range(xs)], axis=0
        )
        y = lax.rem(lax.broadcasted_iota(i32, (rows, 128), 0), ys)
        around = around + jnp.where(y == ys - 1, high_y, pltpu.roll(now, rows - 1, 0))
        around = around + jnp.where(y == 0, low_y, pltpu.roll(now, 1, 0))
        z = lax.broadcasted_iota(i32, (rows, 128), 1)
        around = around + jnp.where(z == 127, 0.0, pltpu.roll(now, 127, 1))
        around = around + jnp.where(z == 0, 0.0, pltpu.roll(now, 1, 1))
        return (
            now
            + thermal_diffusion * (around - 6.0 * now)
            + damping_contribution * (fine[...] - now)
        )

    def dissipate():
        chi[...] = decay[...] * (1.0 + 0.5 * jnp.tanh(grid[...]))

    state[0, core, pair, gx] = state0[...]
    launch(leg(0, 0))
    send_halo(0)
    dissipate()
    total[...] = jnp.zeros_like(total)
    cells = (jnp.int32(0),) * OWNED
    cells = lax.fori_loop(0, turns // 2, first_turn, cells)
    arrive(leg(0, 0))
    launch(leg(0, 1))
    cells = lax.fori_loop(turns // 2, turns, first_turn, cells)
    arrive(leg(0, 1))
    launch(leg(0, 2))
    sums = reduce_sums(0)
    arrive(leg(0, 2))
    now = advance(0, sums, cells)
    state[1, core, pair, gx] = now
    refine(0)
    launch(leg(1, 0))
    after = diffuse(0)
    grid[...] = after

    send_halo(1)
    dissipate()
    arrive(leg(1, 0))
    launch(leg(1, 1))
    total[...] = jnp.zeros_like(total)
    lax.fori_loop(0, turns, second_turn, 0)
    arrive(leg(1, 1))
    launch(leg(1, 2))
    sums = reduce_sums(1)
    arrive(leg(1, 2))
    advance(1, sums, cells)
    refine(1)
    thermal_out[...] = diffuse(1)

    for copy in pending:
        copy.wait_send()


def shards(
    thermal_grid,
    average_blend_fraction,
    normalized_blend_variance,
    small_volume_mass,
    bare_scalar_decay,
    parent_block,
    species_given_block,
    block_position,
    face_partners,
    reaction_increments,
    chemical_coupling,
    species_thermal_weight,
):
    gxn, gyn = lax.axis_size("gx"), lax.axis_size("gy")
    ndev = gxn * gyn
    blocks = block_position.shape[0]
    xs, ys, zs = thermal_grid.shape
    rows = xs * ys
    turns = rows // ROWS
    assert blocks == ndev * OWNED and zs == 128 and rows % (2 * ROWS) == 0
    legs = gxn - 1 + gyn // 2 - 1 + 1
    vmem = pl.BlockSpec(memory_space=pltpu.VMEM)
    smem = pl.BlockSpec(memory_space=pltpu.SMEM)
    dma = pltpu.SemaphoreType.DMA
    species, thermal = pl.pallas_call(
        functools.partial(kernel, gxn, gyn, xs, ys),
        out_shape=(
            jax.ShapeDtypeStruct((OWNED * SPEC, ETA), f32),
            jax.ShapeDtypeStruct((rows, zs), f32),
        ),
        in_specs=[vmem] * 10 + [smem] * 3,
        out_specs=(vmem, vmem),
        scratch_shapes=[
            pltpu.VMEM((ndev, 8, 128), i32),
            pltpu.VMEM((ETA, 128), f32),
            pltpu.VMEM((ETA, 128), f32),
            pltpu.VMEM((rows, zs), f32),
            pltpu.VMEM((rows, zs), f32),
            pltpu.VMEM((rows, zs), f32),
            pltpu.VMEM((rows, zs), f32),
            pltpu.VMEM((rows, zs), f32),
            pltpu.VMEM((turns, ETA, ROWS * 128), f32),
            pltpu.VMEM((turns, ETA, ROWS * 128), bf16),
            pltpu.VMEM((ndev * 8, ETA), f32),
            pltpu.VMEM((STEPS, ndev, 8, ETA), f32),
            pltpu.VMEM((STEPS, ndev, 8, ETA), f32),
            pltpu.VMEM((STEPS, ndev, 8, ETA), f32),
            pltpu.VMEM((STEPS, 2, gyn // 2, gxn, OWNED * SPEC, ETA), f32),
            pltpu.VMEM((STEPS, 2, ys, zs), f32),
            pltpu.VMEM((STEPS, 2, 2 * xs, zs), f32),
            pltpu.VMEM((STEPS, 2 * xs, zs), f32),
            dma((STEPS,)),
            dma((STEPS,)),
            dma((STEPS,)),
            dma((STEPS,)),
            dma((STEPS, legs)),
            dma((STEPS, legs)),
            dma((STEPS, 4)),
            dma((STEPS, 4)),
        ],
        compiler_params=pltpu.CompilerParams(
            collective_id=0, has_side_effects=True, vmem_limit_bytes=48 * 1024 * 1024
        ),
    )(
        thermal_grid.reshape(rows, zs),
        average_blend_fraction.reshape(rows, zs),
        normalized_blend_variance.reshape(rows, zs),
        small_volume_mass.reshape(rows, zs),
        bare_scalar_decay.reshape(rows, zs),
        parent_block.reshape(rows, zs),
        species_given_block.reshape(OWNED * SPEC, ETA),
        block_position.reshape(1, blocks),
        chemical_coupling,
        species_thermal_weight.reshape(1, SPEC),
        block_position,
        face_partners.reshape(-1),
        reaction_increments,
    )
    return (species.reshape(OWNED, SPEC, ETA), thermal.reshape(xs, ys, zs))


def solution(mesh):
    fine = P("gx", "gy", None)
    return jax.shard_map(
        shards,
        mesh=mesh,
        in_specs=(fine,) * 6 + (P(("gx", "gy"), None, None),) + (P(),) * 5,
        out_specs=(P(("gx", "gy"), None, None), fine),
        check_vma=False,
    )
```

time: 601 us -> 76.5 us (0.13)
  waiting for transfers between devices: 280 us -> 0 us
  matrix products: 124 us -> 0 us
  Pallas kernels: 0 us -> 70.4 us
  other arithmetic: 69.2 us -> 0 us
  local copies, waits for them, and re-layouts: 65.2 us -> 5.01 us
  loops' own time: 22.8 us -> 0 us
  starting transfers between devices: 20.9 us -> 0 us
  between operations: 14.3 us -> 0.72 us
    psum x2 -> x0, waiting for transfers between devices: 225 us -> none  [shards(): totals = lax.psum(local_aggregates[position_block_map], ('gx', 'gy'))]
    dot_general x98 -> x0, matrix products: 124 us -> none  [the longest x32 61.6 us: substep(): jnp.einsum('st,ctk->csk', chemical_coupling, jnp.tanh(current), precision...]
    pallas_call x0 -> x1, Pallas kernels: none -> 70.4 us  [shards(): pl.pallas_call(functools.partial(kernel, gxn, gyn, xs, ys), out_shape=(ja...]
    all_gather x1 -> x0, waiting for transfers between devices: 54.5 us -> none  [shards(): lax.all_gather(species_given_block, ('gx', 'gy'), axis=0, tiled=True)]
    mul x65 -> x0, other arithmetic: 37 us -> none  [the longest x32 36.6 us: attach_block(): values = jnp.concatenate([weighted, weighted * speed_piece], axis=-1)]
    dynamic_slice x97 -> x0, local copies, waits for them, and re-layouts: 23.4 us -> none  [the longest x96 22.7 us: small_volume_accumulations(): lax.scan(attach_block, start_total, (flat_table, flat_mass, flat_speed, f...]
    another operation x6 -> x0, loops' own time: 22.8 us -> none  [the longest x2 20.3 us: coarse_advance(): return lax.fori_loop(0, turns, substep, fluid_condition)]
    ppermute x8 -> x0, starting transfers between devices: 20.8 us -> none  [the longest x4 15.6 us: with_halo(): lax.ppermute(lax.slice_in_dim(block, block.shape[dim] - width, None, axis...]
  transfers between devices with their start and end apart: 11 -> 0, of which waited for: 3 -> 0; matrix products, arithmetic and copies ran while one was open for 7% -> 0% of each run, Pallas kernels for 0% -> 0%
where the time goes in v1:
time: 76.5 us; the launch traced here: 76.1 us
  Pallas kernels  70.4 us (92%)
  local copies, waits for them, and re-layouts  5.01 us (7%)
    pallas_call x1, Pallas kernels, shards(): pl.pallas_call(functools.partial(kernel, gxn, gyn, xs, ys), out_shape=(ja...  70.4 us
    unnamed x27, local copies, waits for them, and re-layouts  4.88 us

profile of v1, /device:TPU:0, one launch (start us, length us, event | category | flops | bytes accessed | tf_op | source)
XLA Modules:
  0.0 76.1 jit_solution(5116162984670323462)
XLA Ops:
  0.6 0.0 copy-start.11
  0.6 0.0 copy-start.8
  0.7 0.0 copy-start.9
  0.7 0.0 copy-start.10
  0.7 0.6 copy-done.11
  1.3 0.0 copy-start.2
  1.3 0.0 copy-start.3
  1.3 0.0 copy-start.7
  1.3 0.1 copy.14
  1.4 0.0 copy-start
  1.4 0.0 copy-start.1
  1.5 0.1 reshape.49.partners
  1.6 0.0 copy-done.8
  1.6 0.0 copy-done.9
  1.6 0.0 copy-done.10
  1.6 0.5 copy-done.2
  2.1 0.0 copy-done.3
  2.1 0.0 copy-done.7
  2.1 0.1 copy-done
  2.2 0.0 copy-done.1
  2.2 0.0 copy-start.4
  2.2 0.8 copy-done.4
  3.0 0.0 copy-start.5
  3.0 0.8 copy-done.5
  3.7 0.0 copy-start.6
  3.7 0.8 copy-done.6
  4.5 70.4 %shard_map.131 = (f32[64,128]{1,0:T(8,128)S(1)}, f32[64,128]{1,0:T(8,128)S(1)}) custom-call(f32[64,128]{1,0:T(8,128)S(1)} %bitcast.13, f32[64,128]{1,0:T(8,128)S(1)} %bitcast.14, f32[64,128]{1,0:T(8,128)S(1)} %bitcast.15, f32[64,128]{1,0:T(8,128)S(1)} %bitcast.16, f32[64,128]{1,0:T(8,128)S(1)} %bitcast.17, s32[64,128]{1,0:T(8,128)S(1)} %bitcast.18, ...), custom_call_target="tpu_custom_call" | custom-call | tf_op jit(solution)/shard_map/pallas_call | solution.py:411
  74.9 0.6 copy.17
  75.5 0.6 copy.18
Async XLA Ops:
  0.6 0.7 copy-start.11
  0.6 1.0 %copy-start.8 = (s32[128]{0:T(128)S(1)}, s32[128]{0:T(128)}, u32[]{:S(2)}) copy-start(s32[128]{0:T(128)} %position.1) | copy-start | bytes 1540
  0.7 1.0 %copy-start.9 = (f32[16]{0:T(128)S(1)}, f32[16]{0:T(128)}, u32[]{:S(2)}) copy-start(f32[16]{0:T(128)} %param.23) | copy-start | bytes 196
  0.7 1.0 %copy-start.10 = (s32[128]{0:T(128)S(1)}, s32[128]{0:T(128)}, u32[]{:S(2)}) copy-start(s32[128]{0:T(128)} %increments.1) | copy-start | bytes 1540
  1.3 0.8 copy-start.2
  1.3 0.8 %copy-start.3 = (f32[4,16,128]{2,1,0:T(8,128)S(1)}, f32[4,16,128]{2,1,0:T(8,128)}, u32[]{:S(2)}) copy-start(f32[4,16,128]{2,1,0:T(8,128)} %param.15) | copy-start | bytes 98308
  1.3 0.8 %copy-start.7 = (f32[16,16]{1,0:T(8,128)S(1)}, f32[16,16]{1,0:T(8,128)}, u32[]{:S(2)}) copy-start(f32[16,16]{1,0:T(8,128)} %chem.1) | copy-start | bytes 3076
  1.4 0.8 %copy-start = (f32[4,16,128]{2,1,0:T(8,128)S(1)}, f32[4,16,128]{2,1,0:T(8,128)}, u32[]{:S(2)}) copy-start(f32[4,16,128]{2,1,0:T(8,128)} %param.12) | copy-start | bytes 98308
  1.4 0.8 %copy-start.1 = (f32[4,16,128]{2,1,0:T(8,128)S(1)}, f32[4,16,128]{2,1,0:T(8,128)}, u32[]{:S(2)}) copy-start(f32[4,16,128]{2,1,0:T(8,128)} %param.13) | copy-start | bytes 98308
  2.2 0.8 copy-start.4
  3.0 0.8 copy-start.5
  3.7 0.8 copy-start.6

commit v2 on v1

--- a/solution.py
+++ b/solution.py
@@ -11,8 +11,9 @@
 SPEC = 16
 SUBMAX = 16
 STEPS = 2
-ROWS = 4
+ROWS = 8
 OWNED = 4
+NAMED = 48
 
 coupling = 0.05
 mixing_rate = 0.2
@@ -30,10 +31,12 @@
 
 def kernel(
     gxn, gyn, xs, ys,
+    thermal_in, mean_in, variance_in, mass_in, decay_in, parent_in, state0_in, position_row_in,
+    chem_in, weight_in, position_in, partners_in, increments_in,
+    species_out, thermal_out,
     thermal, mean, variance, mass, decay, parent, state0, position_row, chem, weight,
-    position, partners, increments,
-    species_out, thermal_out,
-    ids, log_a, log_b, shape_a, shape_b, chi, grid, fine, table, table16, total,
+    position, partners, increments, load,
+    ids, names, names_row, bent_rows, columns, weights_known, log_a, log_b, shape_a, shape_b, chi, grid, fine, table, table16, total,
     sent, got, theta, state, face_x, face_y, own_y,
     sums_send, sums_recv, theta_send, theta_recv, state_send, state_recv, halo_send, halo_recv,
 ):
@@ -56,13 +59,50 @@
     def _(j):
         pl.semaphore_signal(barrier, inc=1, device_id=place(me + j), device_id_type=MESH)
 
+    loads = [
+        pltpu.make_async_copy(source, target, load.at[n])
+        for n, (source, target) in enumerate((
+            (position_row_in, position_row), (parent_in, parent), (variance_in, variance),
+            (mean_in, mean), (thermal_in, thermal), (mass_in, mass), (decay_in, decay),
+            (state0_in, state0), (chem_in, chem), (weight_in, weight),
+            (position_in, position), (partners_in, partners), (increments_in, increments),
+        ))
+    ]
+    for copy in loads:
+        copy.start()
+    for copy in loads:
+        copy.wait()
+
     row = lax.broadcasted_iota(i32, (ndev * 8, blocks), 0)
     device = me - (row >> 3)
     slot = jnp.where(device < 0, device + ndev, device) * OWNED + (row & 3)
     hit = position_row[...] == slot
     cell = lax.broadcasted_iota(i32, (ndev * 8, blocks), 1).astype(f32)
     named = jnp.sum(jnp.where(hit, cell, 0.0), axis=1, keepdims=True).astype(i32)
-    ids[...] = jnp.broadcast_to(named, (ndev * 8, 128)).reshape(ndev, 8, 128)
+    ids[...] = jnp.broadcast_to(named, (ndev * 8, 128))
+
+    coarse = lax.broadcasted_iota(i32, (blocks, 128), 0)
+
+    def look(i, seen):
+        for n in range(8):
+            seen = jnp.where(parent[pl.ds(i * 8 + n, 1), :] == coarse, 1.0, seen)
+        return seen
+
+    seen = lax.fori_loop(0, rows // 8, look, jnp.zeros((blocks, 128), f32))
+    seen = jnp.broadcast_to(jnp.max(seen, axis=1, keepdims=True), (blocks, 128))
+    below = (
+        lax.broadcasted_iota(i32, (blocks, blocks), 1)
+        < lax.broadcasted_iota(i32, (blocks, blocks), 0)
+    )
+    rank = jnp.dot(
+        jnp.where(below, 1.0, 0.0).astype(bf16), seen.astype(bf16), preferred_element_type=f32
+    )
+    lanes = lax.broadcasted_iota(i32, (1, 128), 1)
+    wanted = jnp.where(lanes < NAMED, lanes, jnp.where(lanes < 2 * NAMED, lanes - NAMED, -1))
+    match = (rank == wanted.astype(f32)) & (seen > 0.0)
+    list_row = jnp.sum(jnp.where(match, coarse.astype(f32) + 1.0, 0.0), axis=0, keepdims=True) - 1.0
+    names_row[...] = jnp.broadcast_to(list_row, (8, 128)).astype(i32)
+    names[...] = jnp.broadcast_to(list_row, (128, 128)).T[:NAMED].astype(i32)
 
     points = (lax.broadcasted_iota(i32, (ETA, 128), 0).astype(f32) + 0.5) / ETA
     log_a[...] = jnp.log(points)
@@ -76,15 +116,8 @@
         (lax.broadcasted_iota(i32, (OWNED * SPEC, SPEC), 0) & (SPEC - 1))
         == lax.broadcasted_iota(i32, (OWNED * SPEC, SPEC), 1)
     ).astype(f32)
-    wide = jnp.dot(spread, chem[...], precision=HIGHEST, preferred_element_type=f32)
-    wide = lax.dot_general(wide, spread, NT, precision=HIGHEST, preferred_element_type=f32)
-    same = (lax.broadcasted_iota(i32, wide.shape, 0) >> 4) == (
-        lax.broadcasted_iota(i32, wide.shape, 1) >> 4
-    )
-    wide = jnp.where(same, wide, 0.0)
-    wide_high = wide.astype(bf16)
-    wide_low = (wide - wide_high.astype(f32)).astype(bf16)
-    chem_all = jnp.concatenate([wide_high, wide_low], axis=0)
+    for t in range(SPEC):
+        columns[t] = jnp.broadcast_to(chem[:, t : t + 1], (SPEC, 128))
 
     weights = lax.dot_general(
         jnp.broadcast_to(weight[...], (8, SPEC)), spread, NT,
@@ -197,16 +230,31 @@
         whole.wait_recv()
 
     half_row = lax.broadcasted_iota(i32, (8, 128), 0) < 4
-
-    def gather_row(r):
+    upper = (lax.broadcasted_iota(i32, (ndev * 8, 128), 0) & 4) == 0
+
+    def split(values):
+        high = values.astype(bf16)
+        return [high, (values - high.astype(f32)).astype(bf16)]
+
+    def same_cell():
+        return ids[...] == names_row[0:1, :]
+
+    def hits(r):
+        return parent[pl.ds(r, 1), :] == names[...]
+
+    def gather_row(r, first):
+        hit = hits(r)
         here = mass[pl.ds(r, 1), :]
-        both = jnp.where(half_row, here, here * chi[pl.ds(r, 1), :])
-        chosen = jnp.where(parent[pl.ds(r, 1), :][None] == ids[...], both[None], 0.0)
-        return chosen.reshape(ndev * 8, 128).astype(bf16)
-
-    def add_up(i, chosen, values):
-        total[...] += lax.dot_general(
-            jnp.concatenate(chosen, axis=1), values, NT, preferred_element_type=f32
+        parts = [jnp.where(hit, here * chi[pl.ds(r, 1), :], 0.0).astype(bf16)]
+        if first:
+            parts = [jnp.where(hit, here, 0.0).astype(bf16)] + parts
+        return jnp.concatenate(parts, axis=0)
+
+    def add_up(chosen, values):
+        chosen = jnp.concatenate(chosen, axis=1)
+        count = chosen.shape[0]
+        total[128 - 32 - count : 96] += lax.dot_general(
+            chosen, values, NT, preferred_element_type=f32
         )
 
     def first_turn(i, cells):
@@ -218,8 +266,8 @@
             part = raised * (1.0 / jnp.sum(raised, axis=0, keepdims=True))
             table[i, :, n * 128 : (n + 1) * 128] = part
             table16[i, :, n * 128 : (n + 1) * 128] = part.astype(bf16)
-            chosen.append(gather_row(r))
-        add_up(i, chosen, table16[i])
+            chosen.append(gather_row(r, True))
+        add_up(chosen, table16[i])
         each = blocks // turns
         for n in range(each):
             c = i * each + n
@@ -230,11 +278,18 @@
         return cells
 
     def second_turn(i, carry):
-        add_up(i, [gather_row(i * ROWS + n) for n in range(ROWS)], table16[i])
+        add_up([gather_row(i * ROWS + n, False) for n in range(ROWS)], table16[i])
         return carry
 
     def reduce_sums(turn):
-        sent[turn] = total[...].reshape(ndev, 8, 128)
+        lane_low = lax.broadcasted_iota(i32, (ndev * 8, 128), 1) < NAMED
+        pick = jnp.where(same_cell() & (lane_low == upper), 1.0, 0.0).astype(bf16)
+        sums = jnp.dot(
+            jnp.concatenate([pick, pick], axis=1),
+            jnp.concatenate(split(total[...]), axis=0),
+            preferred_element_type=f32,
+        )
+        sent[turn] = sums.reshape(ndev, 8, 128)
         exchange(lambda j: sent.at[turn, j], got, turn, -1, sums_send, sums_recv)
         return sent[turn, 0] + jnp.sum(got[turn, pl.ds(1, ndev - 1)], axis=0)
 
@@ -246,7 +301,9 @@
     lane = lax.broadcasted_iota(i32, (OWNED * SPEC, 128), 1)
 
     def advance(turn, sums, cells):
-        cchi = (sums[4:8] + prior_flux) / (sums[0:4] + prior_weight)
+        if turn == 0:
+            weights_known[...] = sums
+        cchi = (sums[4:8] + prior_flux) / (weights_known[0:4] + prior_weight)
         cchi = spread_rows([cchi[q : q + 1] for q in range(OWNED)])
         counts = jnp.concatenate(
             [jnp.full((SPEC, 128), increments[cells[q]] + 1, i32) for q in range(OWNED)], axis=0
@@ -258,7 +315,7 @@
         for q in range(OWNED):
             around = None
             for j in range(6):
-                near = position[partners[cells[q] * 6 + j]]
+                near = position[partners[cells[q], j]]
                 d = near >> 2
                 y = lax.rem(d, gyn)
                 there = state[
@@ -271,14 +328,14 @@
         now = now + coupling * (around - 6.0 * now)
 
         def substep(index, current):
-            bent = jnp.tanh(current)
-            high = bent.astype(bf16)
-            low = (bent - high.astype(f32)).astype(bf16)
-            source = jnp.dot(
-                chem_all, jnp.concatenate([high, low], axis=1), preferred_element_type=f32
-            )
-            n = OWNED * SPEC
-            source = source[:n, :128] + (source[:n, 128:] + source[n:, :128])
+            bent_rows[...] = jnp.tanh(current)
+            sources = [None] * OWNED
+            for t in range(SPEC):
+                column = columns[t]
+                for q in range(OWNED):
+                    term = column * bent_rows[q * SPEC + t : q * SPEC + t + 1, :]
+                    sources[q] = term if t == 0 else sources[q] + term
+            source = jnp.concatenate(sources, axis=0)
             left = jnp.where(lane == 0, current, pltpu.roll(current, 1, 1))
             right = jnp.where(lane == 127, current, pltpu.roll(current, 127, 1))
             update = mixed * (right - 2.0 * current + left) + reacted * source
@@ -291,18 +348,25 @@
 
     def refine(turn):
         exchange(lambda j: theta.at[turn, 0], theta, turn, 1, theta_send, theta_recv)
-        whole = theta[turn]
+        if turn == 0:
+            launch(leg(1, 0))
+        flat = theta[turn].reshape(ndev * 8, 128).T
+        pick = jnp.where(same_cell() & upper, 1.0, 0.0).astype(bf16)
+        whole = jnp.dot(
+            jnp.concatenate(split(flat), axis=1),
+            jnp.concatenate([pick, pick], axis=0),
+            preferred_element_type=f32,
+        )
         high = whole.astype(bf16).astype(f32)
-        halves = jnp.where(half_row[None], high, whole - high).reshape(ndev * 8, 128)
-        halves = halves.T.astype(bf16)
+        lanes_all = lax.broadcasted_iota(i32, (ETA, 128), 1)
+        halves = jnp.where(lanes_all < NAMED, high, whole - high).astype(bf16)
+        blank = jnp.zeros((128 - 2 * NAMED, 128), bf16)
 
         def body(i, carry):
-            picks = [
-                jnp.where(parent[pl.ds(i * ROWS + n, 1), :][None] == ids[...], 1.0, 0.0)
-                .reshape(ndev * 8, 128)
-                .astype(bf16)
-                for n in range(ROWS)
-            ]
+            picks = []
+            for n in range(ROWS):
+                hit = jnp.where(hits(i * ROWS + n), 1.0, 0.0).astype(bf16)
+                picks.append(jnp.concatenate([hit, hit, blank], axis=0))
             picked = jnp.dot(
                 halves, jnp.concatenate(picks, axis=1), preferred_element_type=f32
             )
@@ -361,14 +425,12 @@
     now = advance(0, sums, cells)
     state[1, core, pair, gx] = now
     refine(0)
-    launch(leg(1, 0))
-    after = diffuse(0)
-    grid[...] = after
+    arrive(leg(1, 0))
+    launch(leg(1, 1))
+    grid[...] = diffuse(0)
 
     send_halo(1)
     dissipate()
-    arrive(leg(1, 0))
-    launch(leg(1, 1))
     total[...] = jnp.zeros_like(total)
     lax.fori_loop(0, turns, second_turn, 0)
     arrive(leg(1, 1))
@@ -406,7 +468,6 @@
     assert blocks == ndev * OWNED and zs == 128 and rows % (2 * ROWS) == 0
     legs = gxn - 1 + gyn // 2 - 1 + 1
     vmem = pl.BlockSpec(memory_space=pltpu.VMEM)
-    smem = pl.BlockSpec(memory_space=pltpu.SMEM)
     dma = pltpu.SemaphoreType.DMA
     species, thermal = pl.pallas_call(
         functools.partial(kernel, gxn, gyn, xs, ys),
@@ -414,10 +475,25 @@
             jax.ShapeDtypeStruct((OWNED * SPEC, ETA), f32),
             jax.ShapeDtypeStruct((rows, zs), f32),
         ),
-        in_specs=[vmem] * 10 + [smem] * 3,
+        in_specs=[pl.BlockSpec(memory_space=pltpu.HBM)] * 13,
         out_specs=(vmem, vmem),
         scratch_shapes=[
-            pltpu.VMEM((ndev, 8, 128), i32),
+            *[pltpu.VMEM((rows, zs), f32)] * 5,
+            pltpu.VMEM((rows, zs), i32),
+            pltpu.VMEM((OWNED * SPEC, ETA), f32),
+            pltpu.VMEM((1, blocks), i32),
+            pltpu.VMEM((SPEC, SPEC), f32),
+            pltpu.VMEM((1, SPEC), f32),
+            pltpu.SMEM((blocks,), i32),
+            pltpu.SMEM((blocks, 6), i32),
+            pltpu.SMEM((blocks,), i32),
+            dma((13,)),
+            pltpu.VMEM((ndev * 8, 128), i32),
+            pltpu.VMEM((NAMED, 128), i32),
+            pltpu.VMEM((8, 128), i32),
+            pltpu.VMEM((OWNED * SPEC, ETA), f32),
+            pltpu.VMEM((SPEC, SPEC, ETA), f32),
+            pltpu.VMEM((8, ETA), f32),
             pltpu.VMEM((ETA, 128), f32),
             pltpu.VMEM((ETA, 128), f32),
             pltpu.VMEM((rows, zs), f32),
@@ -427,7 +503,7 @@
             pltpu.VMEM((rows, zs), f32),
             pltpu.VMEM((turns, ETA, ROWS * 128), f32),
             pltpu.VMEM((turns, ETA, ROWS * 128), bf16),
-            pltpu.VMEM((ndev * 8, ETA), f32),
+            pltpu.VMEM((128, ETA), f32),
             pltpu.VMEM((STEPS, ndev, 8, ETA), f32),
             pltpu.VMEM((STEPS, ndev, 8, ETA), f32),
             pltpu.VMEM((STEPS, ndev, 8, ETA), f32),
@@ -459,7 +535,7 @@
         chemical_coupling,
         species_thermal_weight.reshape(1, SPEC),
         block_position,
-        face_partners.reshape(-1),
+        face_partners,
         reaction_increments,
     )
     return (species.reshape(OWNED, SPEC, ETA), thermal.reshape(xs, ys, zs))

time: 76.5 us -> 70.7 us (0.924)
  Pallas kernels: 70.4 us -> 63 us
  local copies, waits for them, and re-layouts: 5.01 us -> 6.45 us
    pallas_call x1, Pallas kernels: 70.4 us -> 63 us  [shards(): pl.pallas_call(functools.partial(kernel, gxn, gyn, xs, ys), out_shape=(ja...]
    unnamed x27, local copies, waits for them, and re-layouts: 4.88 us -> 6.45 us
where the time goes in v2:
time: 70.7 us; the launch traced here: 70.1 us
  Pallas kernels  63 us (89%)
  local copies, waits for them, and re-layouts  6.45 us (9%)
    pallas_call x1, Pallas kernels, shards(): pl.pallas_call(functools.partial(kernel, gxn, gyn, xs, ys), out_shape=(ja...  63 us
    unnamed x27, local copies, waits for them, and re-layouts  6.45 us

profile of v2, /device:TPU:0, one launch (start us, length us, event | category | flops | bytes accessed | tf_op | source)
XLA Modules:
  0.0 70.1 jit_solution(17903195455478808494)
XLA Ops:
  0.6 0.0 copy-start.11
  0.6 0.0 copy-start.7
  0.7 0.7 copy-done.11
  1.3 0.0 copy-start
  1.3 0.0 copy-start.1
  1.3 0.0 copy-start.8
  1.3 0.0 copy-start.9
  1.3 0.0 copy-start.10
  1.3 0.1 copy.14.partners_in
  1.5 0.0 copy-done.7
  1.5 0.6 copy-done
  2.1 0.0 copy-done.1
  2.1 0.0 copy-done.8
  2.1 0.0 copy-done.9
  2.1 0.0 copy-done.10
  2.1 0.0 copy-start.2
  2.1 0.8 %copy-done.2 = f32[4,16,128]{2,1,0:T(8,128)S(1)} copy-done((f32[4,16,128]{2,1,0:T(8,128)S(1)}, f32[4,16,128]{2,1,0:T(8,128)}, u32[]{:S(2)}) %copy-start.2) | copy-done | bytes 32792
  2.9 0.0 copy-start.3
  2.9 0.8 %copy-done.3 = f32[4,16,128]{2,1,0:T(8,128)S(1)} copy-done((f32[4,16,128]{2,1,0:T(8,128)S(1)}, f32[4,16,128]{2,1,0:T(8,128)}, u32[]{:S(2)}) %copy-start.3) | copy-done | bytes 32792
  3.6 0.0 copy-start.4
  3.6 0.8 %copy-done.4 = f32[4,16,128]{2,1,0:T(8,128)S(1)} copy-done((f32[4,16,128]{2,1,0:T(8,128)S(1)}, f32[4,16,128]{2,1,0:T(8,128)}, u32[]{:S(2)}) %copy-start.4) | copy-done | bytes 32792
  4.4 0.0 copy-start.5
  4.4 0.8 %copy-done.5 = s32[4,16,128]{2,1,0:T(8,128)S(1)} copy-done((s32[4,16,128]{2,1,0:T(8,128)S(1)}, s32[4,16,128]{2,1,0:T(8,128)}, u32[]{:S(2)}) %copy-start.5) | copy-done | bytes 32792
  5.1 0.0 copy-start.6
  5.1 0.8 %copy-done.6 = f32[4,16,128]{2,1,0:T(8,128)S(1)} copy-done((f32[4,16,128]{2,1,0:T(8,128)S(1)}, f32[4,16,128]{2,1,0:T(8,128)}, u32[]{:S(2)}) %copy-start.6) | copy-done | bytes 32792
  5.9 63.0 %shard_map.131 = (f32[64,128]{1,0:T(8,128)S(1)}, f32[64,128]{1,0:T(8,128)S(1)}) custom-call(f32[64,128]{1,0:T(8,128)S(1)} %bitcast.11, f32[64,128]{1,0:T(8,128)S(1)} %bitcast.12, f32[64,128]{1,0:T(8,128)S(1)} %bitcast.13, f32[64,128]{1,0:T(8,128)S(1)} %bitcast.14, f32[64,128]{1,0:T(8,128)S(1)} %bitcast.15, s32[64,128]{1,0:T(8,128)S(1)} %bitcast.16, ...), custom_call_target="tpu_custom_call" | custom-call | tf_op jit(solution)/shard_map/pallas_call | solution.py:472
  68.9 0.6 copy.17
  69.5 0.6 copy.18
Async XLA Ops:
  0.6 0.7 copy-start.11
  0.6 0.8 %copy-start.7 = (f32[16,16]{1,0:T(8,128)S(1)}, f32[16,16]{1,0:T(8,128)}, u32[]{:S(2)}) copy-start(f32[16,16]{1,0:T(8,128)} %chem_in.1) | copy-start | bytes 3076
  1.3 0.8 %copy-start = (f32[4,16,128]{2,1,0:T(8,128)S(1)}, f32[4,16,128]{2,1,0:T(8,128)}, u32[]{:S(2)}) copy-start(f32[4,16,128]{2,1,0:T(8,128)} %param.12) | copy-start | bytes 98308
  1.3 0.8 %copy-start.1 = (f32[4,16,128]{2,1,0:T(8,128)S(1)}, f32[4,16,128]{2,1,0:T(8,128)}, u32[]{:S(2)}) copy-start(f32[4,16,128]{2,1,0:T(8,128)} %param.13) | copy-start | bytes 98308
  1.3 0.8 %copy-start.8 = (s32[128]{0:T(128)S(1)}, s32[128]{0:T(128)}, u32[]{:S(2)}) copy-start(s32[128]{0:T(128)} %position_in.1) | copy-start | bytes 1540
  1.3 0.8 %copy-start.9 = (f32[16]{0:T(128)S(1)}, f32[16]{0:T(128)}, u32[]{:S(2)}) copy-start(f32[16]{0:T(128)} %param.23) | copy-start | bytes 196
  1.3 0.8 %copy-start.10 = (s32[128]{0:T(128)S(1)}, s32[128]{0:T(128)}, u32[]{:S(2)}) copy-start(s32[128]{0:T(128)} %increments_in.1) | copy-start | bytes 1540
  2.1 0.8 %copy-start.2 = (f32[4,16,128]{2,1,0:T(8,128)S(1)}, f32[4,16,128]{2,1,0:T(8,128)}, u32[]{:S(2)}) copy-start(f32[4,16,128]{2,1,0:T(8,128)} %param.14) | copy-start | bytes 98308
  2.9 0.8 %copy-start.3 = (f32[4,16,128]{2,1,0:T(8,128)S(1)}, f32[4,16,128]{2,1,0:T(8,128)}, u32[]{:S(2)}) copy-start(f32[4,16,128]{2,1,0:T(8,128)} %param.15) | copy-start | bytes 98308
  3.6 0.8 %copy-start.4 = (f32[4,16,128]{2,1,0:T(8,128)S(1)}, f32[4,16,128]{2,1,0:T(8,128)}, u32[]{:S(2)}) copy-start(f32[4,16,128]{2,1,0:T(8,128)} %param.16) | copy-start | bytes 98308
  4.4 0.8 %copy-start.5 = (s32[4,16,128]{2,1,0:T(8,128)S(1)}, s32[4,16,128]{2,1,0:T(8,128)}, u32[]{:S(2)}) copy-start(s32[4,16,128]{2,1,0:T(8,128)} %param.17) | copy-start | bytes 98308
  5.1 0.8 %copy-start.6 = (f32[4,16,128]{2,1,0:T(8,128)S(1)}, f32[4,16,128]{2,1,0:T(8,128)}, u32[]{:S(2)}) copy-start(f32[4,16,128]{2,1,0:T(8,128)} %param.18) | copy-start | bytes 98308

commit v3 on v2

--- a/solution.py
+++ b/solution.py
@@ -37,17 +37,21 @@
     thermal, mean, variance, mass, decay, parent, state0, position_row, chem, weight,
     position, partners, increments, load,
     ids, names, names_row, bent_rows, columns, weights_known, log_a, log_b, shape_a, shape_b, chi, grid, fine, table, table16, total,
+    known, next_now, next_mixed, next_reacted, next_counts,
     sent, got, theta, state, face_x, face_y, own_y,
-    sums_send, sums_recv, theta_send, theta_recv, state_send, state_recv, halo_send, halo_recv,
+    sums_send, sums_recv, known_send, known_recv, theta_send, theta_recv, state_send, state_recv, halo_send, halo_recv,
 ):
     ndev = gxn * gyn
     blocks = ndev * OWNED
     rows = xs * ys
     turns = rows // ROWS
-    pairs = gyn // 2
+    xn = gyn // 2
+    yn = xn if gxn % xn == 0 else 1
+    zn = gxn // yn
     gx, gy = lax.axis_index("gx"), lax.axis_index("gy")
     me = gx * gyn + gy
-    core, pair = lax.rem(gy, 2), gy // 2
+    core, x = gy & 1, gy >> 1
+    y, z = lax.rem(gx, yn), gx // yn
 
     def place(device):
         device = lax.rem(device + ndev, ndev)
@@ -132,40 +136,43 @@
 
     pending = []
 
-    def along_gx(turn, j):
-        def block(x):
-            return state.at[turn, core, pair, x]
-
-        there = (lax.rem(gx + j, gxn), gy)
-        here = block(gx)
-        come = block(lax.rem(gx - j + gxn, gxn))
-        sems = (state_send.at[turn, j - 1], state_recv.at[turn, j - 1])
+    def hop(dz, dy, dx):
+        def block(z, y, x):
+            return state.at[
+                core, lax.rem(x + xn, xn), lax.rem(z + zn, zn) * yn + lax.rem(y + yn, yn)
+            ]
+
+        if dy == 0 and dx == 0:
+            there = (lax.rem(z + dz, zn) * yn + y, gy)
+            here = block(z, y, x)
+        else:
+            there = (z * yn + lax.rem(y + dy, yn), lax.rem(x + dx, xn) * 2 + core)
+            here = block(z - dz, y, x)
+        come = block(z - dz, y - dy, x - dx)
+        n = (dz * yn + dy) * xn + dx
+        sems = (state_send.at[n], state_recv.at[n])
         return (
             pltpu.make_async_remote_copy(here, here, *sems, there, MESH),
             pltpu.make_async_remote_copy(come, come, *sems, there, MESH),
         )
 
-    def along_pair(turn, j):
-        other = lax.rem(pair + j, pairs)
-        there = (gx, other * 2 + core)
-        here = state.at[turn, core, pair]
-        come = state.at[turn, core, lax.rem(pair - j + pairs, pairs)]
-        sems = (state_send.at[turn, gxn - 2 + j], state_recv.at[turn, gxn - 2 + j])
-        return (
+    square = [(dy, dx) for dy in range(yn) for dx in range(xn) if dy or dx]
+
+    def along_z(dz):
+        return [hop(dz, 0, 0)]
+
+    def over_square(dz):
+        return [hop(dz, dy, dx) for dy, dx in square]
+
+    def across():
+        there = (gx, x * 2 + 1 - core)
+        here = state.at[core]
+        come = state.at[1 - core]
+        sems = (state_send.at[0], state_recv.at[0])
+        return [(
             pltpu.make_async_remote_copy(here, here, *sems, there, MESH),
             pltpu.make_async_remote_copy(come, come, *sems, there, MESH),
-        )
-
-    def across(turn):
-        there = (gx, pair * 2 + 1 - core)
-        here = state.at[turn, core]
-        come = state.at[turn, 1 - core]
-        last = gxn + pairs - 2
-        sems = (state_send.at[turn, last], state_recv.at[turn, last])
-        return (
-            pltpu.make_async_remote_copy(here, here, *sems, there, MESH),
-            pltpu.make_async_remote_copy(come, come, *sems, there, MESH),
-        )
+        )]
 
     def launch(copies):
         for out, _ in copies:
@@ -175,13 +182,6 @@
     def arrive(copies):
         for _, come in copies:
             come.wait_recv()
-
-    def leg(turn, which):
-        if which == 0:
-            return [along_gx(turn, j) for j in range(1, gxn)]
-        if which == 1:
-            return [along_pair(turn, j) for j in range(1, pairs)]
-        return [across(turn)]
 
     def halo(turn):
         low = (lax.rem(gx - 1 + gxn, gxn), gy)
@@ -227,7 +227,7 @@
             rest, rest, send.at[turn], recv.at[turn], place(me + 1), MESH
         )
         pending.append(whole)
-        whole.wait_recv()
+        return whole
 
     half_row = lax.broadcasted_iota(i32, (8, 128), 0) < 4
     upper = (lax.broadcasted_iota(i32, (ndev * 8, 128), 0) & 4) == 0
@@ -290,7 +290,9 @@
             preferred_element_type=f32,
         )
         sent[turn] = sums.reshape(ndev, 8, 128)
-        exchange(lambda j: sent.at[turn, j], got, turn, -1, sums_send, sums_recv)
+        exchange(
+            lambda j: sent.at[turn, j], got, turn, -1, sums_send, sums_recv
+        ).wait_recv()
         return sent[turn, 0] + jnp.sum(got[turn, pl.ds(1, ndev - 1)], axis=0)
 
     def spread_rows(pieces):
@@ -298,12 +300,23 @@
             [jnp.broadcast_to(p, (SPEC, 128)) for p in pieces], axis=0
         )
 
-    lane = lax.broadcasted_iota(i32, (OWNED * SPEC, 128), 1)
-
-    def advance(turn, sums, cells):
+    def block_of(slot):
+        d = slot >> 2
+        at = d & (gyn - 1)
+        return state[at & 1, at >> 1, d // gyn, pl.ds((slot & 3) * SPEC, SPEC), :]
+
+    def laplacian(current):
+        edge = lax.broadcasted_iota(i32, current.shape, 1)
+        left = jnp.where(edge == 0, current, pltpu.roll(current, 1, 1))
+        right = jnp.where(edge == 127, current, pltpu.roll(current, 127, 1))
+        return right - 2.0 * current + left
+
+    def scalar_decay(turn, sums):
         if turn == 0:
             weights_known[...] = sums
-        cchi = (sums[4:8] + prior_flux) / (weights_known[0:4] + prior_weight)
+        return (sums[4:8] + prior_flux) / (weights_known[0:4] + prior_weight)
+
+    def advance(turn, cchi, cells):
         cchi = spread_rows([cchi[q : q + 1] for q in range(OWNED)])
         counts = jnp.concatenate(
             [jnp.full((SPEC, 128), increments[cells[q]] + 1, i32) for q in range(OWNED)], axis=0
@@ -315,12 +328,11 @@
         for q in range(OWNED):
             around = None
             for j in range(6):
-                near = position[partners[cells[q], j]]
-                d = near >> 2
-                y = lax.rem(d, gyn)
-                there = state[
-                    turn, lax.rem(y, 2), y // 2, d // gyn, pl.ds((near & 3) * SPEC, SPEC), :
-                ]
+                if turn == 0:
+                    there = block_of(position[partners[j, cells[q]]])
+                else:
+                    n = (q * 6 + j) * SPEC
+                    there = next_now[n : n + SPEC, :]
                 around = there if around is None else around + there
             parts.append(around)
         around = jnp.concatenate(parts, axis=0)
@@ -336,20 +348,61 @@
                     term = column * bent_rows[q * SPEC + t : q * SPEC + t + 1, :]
                     sources[q] = term if t == 0 else sources[q] + term
             source = jnp.concatenate(sources, axis=0)
-            left = jnp.where(lane == 0, current, pltpu.roll(current, 1, 1))
-            right = jnp.where(lane == 127, current, pltpu.roll(current, 127, 1))
-            update = mixed * (right - 2.0 * current + left) + reacted * source
+            update = mixed * laplacian(current) + reacted * source
             return jnp.where(index < counts, current + update, current)
 
         now = lax.fori_loop(0, SUBMAX, substep, now)
         species_out[...] = now
         theta[turn, 0] = jnp.dot(weights, now, precision=HIGHEST, preferred_element_type=f32)
-        return now
+
+    def advance_near(cells):
+        def prepare(j, carry):
+            for q in range(OWNED):
+                cell = partners[j, cells[q]]
+                slot = position[cell]
+                now = block_of(slot)
+                around = None
+                for k in range(6):
+                    there = block_of(position[partners[k, cell]])
+                    around = there if around is None else around + there
+                d = me - (slot >> 2)
+                d = jnp.where(d < 0, d + ndev, d)
+                counts = jnp.full((SPEC, 128), increments[cell] + 1, i32)
+                fraction = 1.0 / counts.astype(f32)
+                rows_at = pl.ds((q * 6 + j) * SPEC, SPEC)
+                next_now[rows_at, :] = now + coupling * (around - 6.0 * now)
+                next_mixed[rows_at, :] = fraction * mixing_rate * known[0, d, pl.ds(slot & 3, 1), :]
+                next_reacted[rows_at, :] = fraction * react_rate
+                next_counts[rows_at, :] = counts
+            return carry
+
+        lax.fori_loop(0, 6, prepare, 0)
+        high, low = split(chem[...])
+        chem_wide = jnp.concatenate([high, high, low], axis=1)
+
+        def substep(index, carry):
+            current = next_now[...]
+            high, low = split(jnp.tanh(current))
+
+            def side(values):
+                return jnp.concatenate(
+                    [values[n * SPEC : (n + 1) * SPEC] for n in range(6 * OWNED)], axis=1
+                )
+
+            high, low = side(high), side(low)
+            source = jnp.dot(
+                chem_wide, jnp.concatenate([high, low, high], axis=0), preferred_element_type=f32
+            )
+            source = jnp.concatenate(
+                [source[:, n * 128 : (n + 1) * 128] for n in range(6 * OWNED)], axis=0
+            )
+            update = next_mixed[...] * laplacian(current) + next_reacted[...] * source
+            next_now[...] = jnp.where(index < next_counts[...], current + update, current)
+            return carry
+
+        lax.fori_loop(0, SUBMAX, substep, 0)
 
     def refine(turn):
-        exchange(lambda j: theta.at[turn, 0], theta, turn, 1, theta_send, theta_recv)
-        if turn == 0:
-            launch(leg(1, 0))
         flat = theta[turn].reshape(ndev * 8, 128).T
         pick = jnp.where(same_cell() & upper, 1.0, 0.0).astype(bf16)
         whole = jnp.dot(
@@ -408,36 +461,42 @@
     def dissipate():
         chi[...] = decay[...] * (1.0 + 0.5 * jnp.tanh(grid[...]))
 
-    state[0, core, pair, gx] = state0[...]
-    launch(leg(0, 0))
+    state[core, x, gx] = state0[...]
+    for dz in range(1, zn):
+        launch(along_z(dz))
+    launch(over_square(0))
     send_halo(0)
     dissipate()
     total[...] = jnp.zeros_like(total)
     cells = (jnp.int32(0),) * OWNED
     cells = lax.fori_loop(0, turns // 2, first_turn, cells)
-    arrive(leg(0, 0))
-    launch(leg(0, 1))
+    for dz in range(1, zn):
+        arrive(along_z(dz))
+        launch(over_square(dz))
     cells = lax.fori_loop(turns // 2, turns, first_turn, cells)
-    arrive(leg(0, 1))
-    launch(leg(0, 2))
     sums = reduce_sums(0)
-    arrive(leg(0, 2))
-    now = advance(0, sums, cells)
-    state[1, core, pair, gx] = now
+    cchi = scalar_decay(0, sums)
+    known[0, 0] = jnp.concatenate([cchi, cchi], axis=0)
+    for dz in range(zn):
+        arrive(over_square(dz))
+    launch(across())
+    all_known = exchange(lambda j: known.at[0, 0], known, 0, 1, known_send, known_recv)
+    arrive(across())
+    advance(0, cchi, cells)
+    moving = exchange(lambda j: theta.at[0, 0], theta, 0, 1, theta_send, theta_recv)
+    all_known.wait_recv()
+    advance_near(cells)
+    moving.wait_recv()
     refine(0)
-    arrive(leg(1, 0))
-    launch(leg(1, 1))
     grid[...] = diffuse(0)
 
     send_halo(1)
     dissipate()
     total[...] = jnp.zeros_like(total)
     lax.fori_loop(0, turns, second_turn, 0)
-    arrive(leg(1, 1))
-    launch(leg(1, 2))
     sums = reduce_sums(1)
-    arrive(leg(1, 2))
-    advance(1, sums, cells)
+    advance(1, scalar_decay(1, sums), cells)
+    exchange(lambda j: theta.at[1, 0], theta, 1, 1, theta_send, theta_recv).wait_recv()
     refine(1)
     thermal_out[...] = diffuse(1)
 
@@ -466,7 +525,6 @@
     rows = xs * ys
     turns = rows // ROWS
     assert blocks == ndev * OWNED and zs == 128 and rows % (2 * ROWS) == 0
-    legs = gxn - 1 + gyn // 2 - 1 + 1
     vmem = pl.BlockSpec(memory_space=pltpu.VMEM)
     dma = pltpu.SemaphoreType.DMA
     species, thermal = pl.pallas_call(
@@ -485,7 +543,7 @@
             pltpu.VMEM((SPEC, SPEC), f32),
             pltpu.VMEM((1, SPEC), f32),
             pltpu.SMEM((blocks,), i32),
-            pltpu.SMEM((blocks, 6), i32),
+            pltpu.SMEM((6, blocks), i32),
             pltpu.SMEM((blocks,), i32),
             dma((13,)),
             pltpu.VMEM((ndev * 8, 128), i32),
@@ -504,24 +562,29 @@
             pltpu.VMEM((turns, ETA, ROWS * 128), f32),
             pltpu.VMEM((turns, ETA, ROWS * 128), bf16),
             pltpu.VMEM((128, ETA), f32),
+            pltpu.VMEM((1, ndev, 8, ETA), f32),
+            *[pltpu.VMEM((6 * OWNED * SPEC, ETA), f32)] * 3,
+            pltpu.VMEM((6 * OWNED * SPEC, ETA), i32),
             pltpu.VMEM((STEPS, ndev, 8, ETA), f32),
             pltpu.VMEM((STEPS, ndev, 8, ETA), f32),
             pltpu.VMEM((STEPS, ndev, 8, ETA), f32),
-            pltpu.VMEM((STEPS, 2, gyn // 2, gxn, OWNED * SPEC, ETA), f32),
+            pltpu.VMEM((2, gyn // 2, gxn, OWNED * SPEC, ETA), f32),
             pltpu.VMEM((STEPS, 2, ys, zs), f32),
             pltpu.VMEM((STEPS, 2, 2 * xs, zs), f32),
             pltpu.VMEM((STEPS, 2 * xs, zs), f32),
             dma((STEPS,)),
             dma((STEPS,)),
+            dma((1,)),
+            dma((1,)),
             dma((STEPS,)),
             dma((STEPS,)),
-            dma((STEPS, legs)),
-            dma((STEPS, legs)),
+            dma((ndev // 2,)),
+            dma((ndev // 2,)),
             dma((STEPS, 4)),
             dma((STEPS, 4)),
         ],
         compiler_params=pltpu.CompilerParams(
-            collective_id=0, has_side_effects=True, vmem_limit_bytes=48 * 1024 * 1024
+            collective_id=0, has_side_effects=True, vmem_limit_bytes=63 * 1024 * 1024
         ),
     )(
         thermal_grid.reshape(rows, zs),
@@ -535,7 +598,7 @@
         chemical_coupling,
         species_thermal_weight.reshape(1, SPEC),
         block_position,
-        face_partners,
+        face_partners.T,
         reaction_increments,
     )
     return (species.reshape(OWNED, SPEC, ETA), thermal.reshape(xs, ys, zs))

time: 70.7 us -> 50.9 us (0.72)
  Pallas kernels: 63 us -> 48 us
  local copies, waits for them, and re-layouts: 6.45 us -> 2 us
    pallas_call x1, Pallas kernels: 63 us -> 48 us  [shards(): pl.pallas_call(functools.partial(kernel, gxn, gyn, xs, ys), out_shape=(ja...]
    unnamed x27 -> x4, local copies, waits for them, and re-layouts: 6.45 us -> 2 us
where the time goes in v3:
time: 50.9 us; the launch traced here: 50.6 us
  Pallas kernels  48 us (94%)
  local copies, waits for them, and re-layouts  2 us (4%)
  between operations  0.65 us (1%)
    pallas_call x1, Pallas kernels, shards(): pl.pallas_call(functools.partial(kernel, gxn, gyn, xs, ys), out_shape=(ja...  48 us
    unnamed x4, local copies, waits for them, and re-layouts  2 us

profile of v3, /device:TPU:0, one launch (start us, length us, event | category | flops | bytes accessed | tf_op | source)
XLA Modules:
  0.0 50.6 jit_solution(5501650946766639627)
XLA Ops:
  0.6 48.0 %shard_map.131 = (f32[64,128]{1,0:T(8,128)}, f32[64,128]{1,0:T(8,128)}) custom-call(f32[64,128]{1,0:T(8,128)} %bitcast.14, f32[64,128]{1,0:T(8,128)} %bitcast.15, f32[64,128]{1,0:T(8,128)} %bitcast.16, f32[64,128]{1,0:T(8,128)} %bitcast.17, f32[64,128]{1,0:T(8,128)} %bitcast.18, s32[64,128]{1,0:T(8,128)} %bitcast.19, f32[64,128]{1,0:T(8,128)} %bitcast.20, ...), custom_call_target="tpu_custom_call" | custom-call | tf_op jit(solution)/shard_map/pallas_call | solution.py:530
  48.6 0.0 copy-start
  48.6 1.4 %copy.16 = f32[4,16,128]{2,1,0:T(8,128)} copy(f32[4,16,128]{2,1,0:T(8,128)} %bitcast.13) | data formatting | bytes 65536
  50.0 0.0 copy-done
  50.0 0.6 %copy.17 = f32[4,16,128]{2,1,0:T(8,128)} copy(f32[4,16,128]{2,1,0:T(8,128)S(1)} %bitcast.12) | data formatting | bytes 65536
Async XLA Ops:
  48.6 1.4 %copy-start = (f32[64,128]{1,0:T(8,128)S(1)}, f32[64,128]{1,0:T(8,128)}, u32[]{:S(2)}) copy-start(f32[64,128]{1,0:T(8,128)} %get-tuple-element.5) | copy-start | bytes 98308

commit v4 on v3

--- a/solution.py
+++ b/solution.py
@@ -36,15 +36,16 @@
     species_out, thermal_out,
     thermal, mean, variance, mass, decay, parent, state0, position_row, chem, weight,
     position, partners, increments, load,
-    ids, names, names_row, bent_rows, columns, weights_known, log_a, log_b, shape_a, shape_b, chi, grid, fine, table, table16, total,
+    ids, names, names_row, bent_rows, columns, weights_known, weights_of, ids_short, log_a, log_b, shape_a, shape_b, chi, grid, fine, table, table16, total,
     known, next_now, next_mixed, next_reacted, next_counts,
-    sent, got, theta, state, face_x, face_y, own_y,
-    sums_send, sums_recv, known_send, known_recv, theta_send, theta_recv, state_send, state_recv, halo_send, halo_recv,
+    sent, got, sent_short, got_short, theta, state, face_x, face_y, own_y,
+    sums_send, sums_recv, short_send, short_recv, known_send, known_recv, theta_send, theta_recv, state_send, state_recv, halo_send, halo_recv,
 ):
     ndev = gxn * gyn
     blocks = ndev * OWNED
     rows = xs * ys
     turns = rows // ROWS
+    unroll = ndev - 1 if ndev <= 32 else 1
     xn = gyn // 2
     yn = xn if gxn % xn == 0 else 1
     zn = gxn // yn
@@ -54,85 +55,90 @@
     y, z = lax.rem(gx, yn), gx // yn
 
     def place(device):
-        device = lax.rem(device + ndev, ndev)
-        return (device // gyn, lax.rem(device, gyn))
+        device = (device + ndev) & (ndev - 1)
+        return (device >> (gyn.bit_length() - 1), device & (gyn - 1))
 
     barrier = pltpu.get_barrier_semaphore()
 
-    @pl.loop(1, ndev)
+    @pl.loop(1, ndev, unroll=unroll)
     def _(j):
         pl.semaphore_signal(barrier, inc=1, device_id=place(me + j), device_id_type=MESH)
 
     loads = [
         pltpu.make_async_copy(source, target, load.at[n])
         for n, (source, target) in enumerate((
-            (position_row_in, position_row), (parent_in, parent), (variance_in, variance),
-            (mean_in, mean), (thermal_in, thermal), (mass_in, mass), (decay_in, decay),
-            (state0_in, state0), (chem_in, chem), (weight_in, weight),
+            (state0_in, state0), (thermal_in, thermal), (position_row_in, position_row),
+            (parent_in, parent), (variance_in, variance), (mean_in, mean), (mass_in, mass),
+            (decay_in, decay), (chem_in, chem), (weight_in, weight),
             (position_in, position), (partners_in, partners), (increments_in, increments),
         ))
     ]
     for copy in loads:
         copy.start()
-    for copy in loads:
-        copy.wait()
-
-    row = lax.broadcasted_iota(i32, (ndev * 8, blocks), 0)
-    device = me - (row >> 3)
-    slot = jnp.where(device < 0, device + ndev, device) * OWNED + (row & 3)
-    hit = position_row[...] == slot
-    cell = lax.broadcasted_iota(i32, (ndev * 8, blocks), 1).astype(f32)
-    named = jnp.sum(jnp.where(hit, cell, 0.0), axis=1, keepdims=True).astype(i32)
-    ids[...] = jnp.broadcast_to(named, (ndev * 8, 128))
-
-    coarse = lax.broadcasted_iota(i32, (blocks, 128), 0)
-
-    def look(i, seen):
-        for n in range(8):
-            seen = jnp.where(parent[pl.ds(i * 8 + n, 1), :] == coarse, 1.0, seen)
-        return seen
-
-    seen = lax.fori_loop(0, rows // 8, look, jnp.zeros((blocks, 128), f32))
-    seen = jnp.broadcast_to(jnp.max(seen, axis=1, keepdims=True), (blocks, 128))
-    below = (
-        lax.broadcasted_iota(i32, (blocks, blocks), 1)
-        < lax.broadcasted_iota(i32, (blocks, blocks), 0)
-    )
-    rank = jnp.dot(
-        jnp.where(below, 1.0, 0.0).astype(bf16), seen.astype(bf16), preferred_element_type=f32
-    )
-    lanes = lax.broadcasted_iota(i32, (1, 128), 1)
-    wanted = jnp.where(lanes < NAMED, lanes, jnp.where(lanes < 2 * NAMED, lanes - NAMED, -1))
-    match = (rank == wanted.astype(f32)) & (seen > 0.0)
-    list_row = jnp.sum(jnp.where(match, coarse.astype(f32) + 1.0, 0.0), axis=0, keepdims=True) - 1.0
-    names_row[...] = jnp.broadcast_to(list_row, (8, 128)).astype(i32)
-    names[...] = jnp.broadcast_to(list_row, (128, 128)).T[:NAMED].astype(i32)
-
-    points = (lax.broadcasted_iota(i32, (ETA, 128), 0).astype(f32) + 0.5) / ETA
-    log_a[...] = jnp.log(points)
-    log_b[...] = jnp.log(1.0 - points)
-    shape_sum = 1.0 / variance[...] - 1.0
-    shape_a[...] = mean[...] * shape_sum - 1.0
-    shape_b[...] = (1.0 - mean[...]) * shape_sum - 1.0
-    grid[...] = thermal[...]
-
-    spread = (
-        (lax.broadcasted_iota(i32, (OWNED * SPEC, SPEC), 0) & (SPEC - 1))
-        == lax.broadcasted_iota(i32, (OWNED * SPEC, SPEC), 1)
-    ).astype(f32)
-    for t in range(SPEC):
-        columns[t] = jnp.broadcast_to(chem[:, t : t + 1], (SPEC, 128))
-
-    weights = lax.dot_general(
-        jnp.broadcast_to(weight[...], (8, SPEC)), spread, NT,
-        precision=HIGHEST, preferred_element_type=f32,
-    )
-    mine = (lax.broadcasted_iota(i32, weights.shape, 0) & 3) == (
-        lax.broadcasted_iota(i32, weights.shape, 1) >> 4
-    )
-    weights = jnp.where(mine, weights, 0.0)
-
+    loads[0].wait()
     pl.semaphore_wait(barrier, ndev - 1)
+
+    def prepare_all():
+        for copy in loads[2:]:
+            copy.wait()
+        def cells_of(count, shift):
+            row = lax.broadcasted_iota(i32, (count, blocks), 0)
+            device = me - (row >> shift)
+            slot = jnp.where(device < 0, device + ndev, device) * OWNED + (row & 3)
+            cell = lax.broadcasted_iota(i32, (count, blocks), 1).astype(f32)
+            found = jnp.where(position_row[...] == slot, cell, 0.0)
+            named = jnp.sum(found, axis=1, keepdims=True).astype(i32)
+            return jnp.broadcast_to(named, (count, 128))
+
+        ids[...] = cells_of(ndev * 8, 3)
+        ids_short[...] = cells_of(ndev * 4, 2)
+
+        coarse = lax.broadcasted_iota(i32, (blocks, 128), 0)
+
+        def look(i, seen):
+            for n in range(8):
+                seen = jnp.where(parent[pl.ds(i * 8 + n, 1), :] == coarse, 1.0, seen)
+            return seen
+
+        seen = lax.fori_loop(0, rows // 8, look, jnp.zeros((blocks, 128), f32))
+        seen = jnp.broadcast_to(jnp.max(seen, axis=1, keepdims=True), (blocks, 128))
+        below = (
+            lax.broadcasted_iota(i32, (blocks, blocks), 1)
+            < lax.broadcasted_iota(i32, (blocks, blocks), 0)
+        )
+        rank = jnp.dot(
+            jnp.where(below, 1.0, 0.0).astype(bf16), seen.astype(bf16), preferred_element_type=f32
+        )
+        lanes = lax.broadcasted_iota(i32, (1, 128), 1)
+        wanted = jnp.where(lanes < NAMED, lanes, jnp.where(lanes < 2 * NAMED, lanes - NAMED, -1))
+        match = (rank == wanted.astype(f32)) & (seen > 0.0)
+        list_row = jnp.sum(jnp.where(match, coarse.astype(f32) + 1.0, 0.0), axis=0, keepdims=True) - 1.0
+        names_row[...] = jnp.broadcast_to(list_row, (8, 128)).astype(i32)
+        names[...] = jnp.broadcast_to(list_row, (128, 128)).T[:NAMED].astype(i32)
+
+        points = (lax.broadcasted_iota(i32, (ETA, 128), 0).astype(f32) + 0.5) / ETA
+        log_a[...] = jnp.log(points)
+        log_b[...] = jnp.log(1.0 - points)
+        shape_sum = 1.0 / variance[...] - 1.0
+        shape_a[...] = mean[...] * shape_sum - 1.0
+        shape_b[...] = (1.0 - mean[...]) * shape_sum - 1.0
+
+        for t in range(SPEC):
+            columns[t] = jnp.broadcast_to(chem[:, t : t + 1], (SPEC, 128))
+
+        spread = (
+            (lax.broadcasted_iota(i32, (OWNED * SPEC, SPEC), 0) & (SPEC - 1))
+            == lax.broadcasted_iota(i32, (OWNED * SPEC, SPEC), 1)
+        ).astype(f32)
+        weights = lax.dot_general(
+            jnp.broadcast_to(weight[...], (OWNED, SPEC)), spread, NT,
+            precision=HIGHEST, preferred_element_type=f32,
+        )
+        mine = lax.broadcasted_iota(i32, weights.shape, 0) == (
+            lax.broadcasted_iota(i32, weights.shape, 1) >> 4
+        )
+        weights = jnp.where(mine, weights, 0.0)
+        weights_of[...] = weights
 
     pending = []
 
@@ -215,7 +221,7 @@
         launch(halo(turn))
 
     def exchange(source, target, turn, sign, send, recv):
-        @pl.loop(1, ndev)
+        @pl.loop(1, ndev, unroll=unroll)
         def _(j):
             pltpu.make_async_remote_copy(
                 source(j), target.at[turn, j], send.at[turn], recv.at[turn],
@@ -235,9 +241,6 @@
     def split(values):
         high = values.astype(bf16)
         return [high, (values - high.astype(f32)).astype(bf16)]
-
-    def same_cell():
-        return ids[...] == names_row[0:1, :]
 
     def hits(r):
         return parent[pl.ds(r, 1), :] == names[...]
@@ -281,19 +284,35 @@
         add_up([gather_row(i * ROWS + n, False) for n in range(ROWS)], table16[i])
         return carry
 
-    def reduce_sums(turn):
-        lane_low = lax.broadcasted_iota(i32, (ndev * 8, 128), 1) < NAMED
-        pick = jnp.where(same_cell() & (lane_low == upper), 1.0, 0.0).astype(bf16)
-        sums = jnp.dot(
+    def pick_sums(pick):
+        pick = jnp.where(pick, 1.0, 0.0).astype(bf16)
+        return jnp.dot(
             jnp.concatenate([pick, pick], axis=1),
             jnp.concatenate(split(total[...]), axis=0),
             preferred_element_type=f32,
         )
-        sent[turn] = sums.reshape(ndev, 8, 128)
-        exchange(
-            lambda j: sent.at[turn, j], got, turn, -1, sums_send, sums_recv
-        ).wait_recv()
-        return sent[turn, 0] + jnp.sum(got[turn, pl.ds(1, ndev - 1)], axis=0)
+
+    def send_sums(turn):
+        if turn == 0:
+            low = lax.broadcasted_iota(i32, (ndev * 8, 128), 1) < NAMED
+            sums = pick_sums((ids[...] == names_row[0:1, :]) & (low == upper))
+            sent[0] = sums.reshape(ndev, 8, 128)
+            return exchange(lambda j: sent.at[0, j], got, 0, -1, sums_send, sums_recv)
+        low = lax.broadcasted_iota(i32, (ndev * 4, 128), 1) < NAMED
+        sums = pick_sums((ids_short[...] == names_row[0:1, :]) & ~low)
+        sent_short[0] = sums.reshape(ndev, 4, 128)
+        return exchange(
+            lambda j: sent_short.at[0, j], got_short, 0, -1, short_send, short_recv
+        )
+
+    def scalar_decay(turn):
+        if turn == 0:
+            sums = sent[0, 0] + jnp.sum(got[0, pl.ds(1, ndev - 1)], axis=0)
+            weights_known[...] = sums[0:4]
+            flux = sums[4:8]
+        else:
+            flux = sent_short[0, 0] + jnp.sum(got_short[0, pl.ds(1, ndev - 1)], axis=0)
+        return (flux + prior_flux) / (weights_known[...] + prior_weight)
 
     def spread_rows(pieces):
         return jnp.concatenate(
@@ -303,18 +322,13 @@
     def block_of(slot):
         d = slot >> 2
         at = d & (gyn - 1)
-        return state[at & 1, at >> 1, d // gyn, pl.ds((slot & 3) * SPEC, SPEC), :]
+        return state[at & 1, at >> 1, d >> (gyn.bit_length() - 1), pl.ds((slot & 3) * SPEC, SPEC), :]
 
     def laplacian(current):
         edge = lax.broadcasted_iota(i32, current.shape, 1)
         left = jnp.where(edge == 0, current, pltpu.roll(current, 1, 1))
         right = jnp.where(edge == 127, current, pltpu.roll(current, 127, 1))
         return right - 2.0 * current + left
-
-    def scalar_decay(turn, sums):
-        if turn == 0:
-            weights_known[...] = sums
-        return (sums[4:8] + prior_flux) / (weights_known[0:4] + prior_weight)
 
     def advance(turn, cchi, cells):
         cchi = spread_rows([cchi[q : q + 1] for q in range(OWNED)])
@@ -353,7 +367,7 @@
 
         now = lax.fori_loop(0, SUBMAX, substep, now)
         species_out[...] = now
-        theta[turn, 0] = jnp.dot(weights, now, precision=HIGHEST, preferred_element_type=f32)
+        theta[turn, 0] = jnp.dot(weights_of[...], now, precision=HIGHEST, preferred_element_type=f32)
 
     def advance_near(cells):
         def prepare(j, carry):
@@ -377,6 +391,8 @@
             return carry
 
         lax.fori_loop(0, 6, prepare, 0)
+
+    def substeps_near(first, last):
         high, low = split(chem[...])
         chem_wide = jnp.concatenate([high, high, low], axis=1)
 
@@ -400,11 +416,11 @@
             next_now[...] = jnp.where(index < next_counts[...], current + update, current)
             return carry
 
-        lax.fori_loop(0, SUBMAX, substep, 0)
+        lax.fori_loop(first, last, substep, 0)
 
     def refine(turn):
-        flat = theta[turn].reshape(ndev * 8, 128).T
-        pick = jnp.where(same_cell() & upper, 1.0, 0.0).astype(bf16)
+        flat = theta[turn].reshape(ndev * 4, 128).T
+        pick = jnp.where(ids_short[...] == names_row[0:1, :], 1.0, 0.0).astype(bf16)
         whole = jnp.dot(
             jnp.concatenate(split(flat), axis=1),
             jnp.concatenate([pick, pick], axis=0),
@@ -465,7 +481,10 @@
     for dz in range(1, zn):
         launch(along_z(dz))
     launch(over_square(0))
+    loads[1].wait()
+    grid[...] = thermal[...]
     send_halo(0)
+    prepare_all()
     dissipate()
     total[...] = jnp.zeros_like(total)
     cells = (jnp.int32(0),) * OWNED
@@ -474,9 +493,9 @@
         arrive(along_z(dz))
         launch(over_square(dz))
     cells = lax.fori_loop(turns // 2, turns, first_turn, cells)
-    sums = reduce_sums(0)
-    cchi = scalar_decay(0, sums)
-    known[0, 0] = jnp.concatenate([cchi, cchi], axis=0)
+    send_sums(0).wait_recv()
+    cchi = scalar_decay(0)
+    known[0, 0] = cchi
     for dz in range(zn):
         arrive(over_square(dz))
     launch(across())
@@ -486,6 +505,7 @@
     moving = exchange(lambda j: theta.at[0, 0], theta, 0, 1, theta_send, theta_recv)
     all_known.wait_recv()
     advance_near(cells)
+    substeps_near(0, SUBMAX // 2)
     moving.wait_recv()
     refine(0)
     grid[...] = diffuse(0)
@@ -494,8 +514,10 @@
     dissipate()
     total[...] = jnp.zeros_like(total)
     lax.fori_loop(0, turns, second_turn, 0)
-    sums = reduce_sums(1)
-    advance(1, scalar_decay(1, sums), cells)
+    moving = send_sums(1)
+    substeps_near(SUBMAX // 2, SUBMAX)
+    moving.wait_recv()
+    advance(1, scalar_decay(1), cells)
     exchange(lambda j: theta.at[1, 0], theta, 1, 1, theta_send, theta_recv).wait_recv()
     refine(1)
     thermal_out[...] = diffuse(1)
@@ -524,6 +546,7 @@
     xs, ys, zs = thermal_grid.shape
     rows = xs * ys
     turns = rows // ROWS
+    assert ndev & (ndev - 1) == 0 and gyn & (gyn - 1) == 0
     assert blocks == ndev * OWNED and zs == 128 and rows % (2 * ROWS) == 0
     vmem = pl.BlockSpec(memory_space=pltpu.VMEM)
     dma = pltpu.SemaphoreType.DMA
@@ -551,7 +574,9 @@
             pltpu.VMEM((8, 128), i32),
             pltpu.VMEM((OWNED * SPEC, ETA), f32),
             pltpu.VMEM((SPEC, SPEC, ETA), f32),
-            pltpu.VMEM((8, ETA), f32),
+            pltpu.VMEM((4, ETA), f32),
+            pltpu.VMEM((OWNED, OWNED * SPEC), f32),
+            pltpu.VMEM((ndev * 4, 128), i32),
             pltpu.VMEM((ETA, 128), f32),
             pltpu.VMEM((ETA, 128), f32),
             pltpu.VMEM((rows, zs), f32),
@@ -562,18 +587,22 @@
             pltpu.VMEM((turns, ETA, ROWS * 128), f32),
             pltpu.VMEM((turns, ETA, ROWS * 128), bf16),
             pltpu.VMEM((128, ETA), f32),
-            pltpu.VMEM((1, ndev, 8, ETA), f32),
+            pltpu.VMEM((1, ndev, 4, ETA), f32),
             *[pltpu.VMEM((6 * OWNED * SPEC, ETA), f32)] * 3,
             pltpu.VMEM((6 * OWNED * SPEC, ETA), i32),
-            pltpu.VMEM((STEPS, ndev, 8, ETA), f32),
-            pltpu.VMEM((STEPS, ndev, 8, ETA), f32),
-            pltpu.VMEM((STEPS, ndev, 8, ETA), f32),
+            pltpu.VMEM((1, ndev, 8, ETA), f32),
+            pltpu.VMEM((1, ndev, 8, ETA), f32),
+            pltpu.VMEM((1, ndev, 4, ETA), f32),
+            pltpu.VMEM((1, ndev, 4, ETA), f32),
+            pltpu.VMEM((STEPS, ndev, 4, ETA), f32),
             pltpu.VMEM((2, gyn // 2, gxn, OWNED * SPEC, ETA), f32),
             pltpu.VMEM((STEPS, 2, ys, zs), f32),
             pltpu.VMEM((STEPS, 2, 2 * xs, zs), f32),
             pltpu.VMEM((STEPS, 2 * xs, zs), f32),
-            dma((STEPS,)),
-            dma((STEPS,)),
+            dma((1,)),
+            dma((1,)),
+            dma((1,)),
+            dma((1,)),
             dma((1,)),
             dma((1,)),
             dma((STEPS,)),

time: 50.9 us -> 46.9 us (0.921)
  Pallas kernels: 48 us -> 44 us
    pallas_call x1, Pallas kernels: 48 us -> 44 us  [shards(): pl.pallas_call(functools.partial(kernel, gxn, gyn, xs, ys), out_shape=(ja...]
where the time goes in v4:
time: 46.9 us; the launch traced here: 46.7 us
  Pallas kernels  44 us (94%)
  local copies, waits for them, and re-layouts  2 us (4%)
  between operations  0.65 us (1%)
    pallas_call x1, Pallas kernels, shards(): pl.pallas_call(functools.partial(kernel, gxn, gyn, xs, ys), out_shape=(ja...  44 us
    unnamed x4, local copies, waits for them, and re-layouts  2 us

profile of v4, /device:TPU:0, one launch (start us, length us, event | category | flops | bytes accessed | tf_op | source)
XLA Modules:
  0.0 46.7 jit_solution(16185812335993291667)
XLA Ops:
  0.6 44.0 %shard_map.131 = (f32[64,128]{1,0:T(8,128)}, f32[64,128]{1,0:T(8,128)}) custom-call(f32[64,128]{1,0:T(8,128)} %bitcast.14, f32[64,128]{1,0:T(8,128)} %bitcast.15, f32[64,128]{1,0:T(8,128)} %bitcast.16, f32[64,128]{1,0:T(8,128)} %bitcast.17, f32[64,128]{1,0:T(8,128)} %bitcast.18, s32[64,128]{1,0:T(8,128)} %bitcast.19, f32[64,128]{1,0:T(8,128)} %bitcast.20, ...), custom_call_target="tpu_custom_call" | custom-call | tf_op jit(solution)/shard_map/pallas_call | solution.py:553
  44.7 0.0 copy-start
  44.7 1.4 %copy.16 = f32[4,16,128]{2,1,0:T(8,128)} copy(f32[4,16,128]{2,1,0:T(8,128)} %bitcast.13) | data formatting | bytes 65536
  46.1 0.0 copy-done
  46.1 0.6 %copy.17 = f32[4,16,128]{2,1,0:T(8,128)} copy(f32[4,16,128]{2,1,0:T(8,128)S(1)} %bitcast.12) | data formatting | bytes 65536
Async XLA Ops:
  44.7 1.4 %copy-start = (f32[64,128]{1,0:T(8,128)S(1)}, f32[64,128]{1,0:T(8,128)}, u32[]{:S(2)}) copy-start(f32[64,128]{1,0:T(8,128)} %get-tuple-element.5) | copy-start | bytes 98308

commit v5 on v4

--- a/solution.py
+++ b/solution.py
@@ -11,7 +11,7 @@
 SPEC = 16
 SUBMAX = 16
 STEPS = 2
-ROWS = 8
+ROWS = 16
 OWNED = 4
 NAMED = 48
 
@@ -33,7 +33,7 @@
     gxn, gyn, xs, ys,
     thermal_in, mean_in, variance_in, mass_in, decay_in, parent_in, state0_in, position_row_in,
     chem_in, weight_in, position_in, partners_in, increments_in,
-    species_out, thermal_out,
+    result,
     thermal, mean, variance, mass, decay, parent, state0, position_row, chem, weight,
     position, partners, increments, load,
     ids, names, names_row, bent_rows, columns, weights_known, weights_of, ids_short, log_a, log_b, shape_a, shape_b, chi, grid, fine, table, table16, total,
@@ -170,11 +170,13 @@
     def over_square(dz):
         return [hop(dz, dy, dx) for dy, dx in square]
 
-    def across():
+    def across(dz):
         there = (gx, x * 2 + 1 - core)
-        here = state.at[core]
-        come = state.at[1 - core]
-        sems = (state_send.at[0], state_recv.at[0])
+        part = pl.ds(lax.rem(z - dz + zn, zn) * yn, yn)
+        here = state.at[core, :, part]
+        come = state.at[1 - core, :, part]
+        n = yn * xn * zn + dz
+        sems = (state_send.at[n], state_recv.at[n])
         return [(
             pltpu.make_async_remote_copy(here, here, *sems, there, MESH),
             pltpu.make_async_remote_copy(come, come, *sems, there, MESH),
@@ -350,7 +352,7 @@
                 around = there if around is None else around + there
             parts.append(around)
         around = jnp.concatenate(parts, axis=0)
-        now = state0[...] if turn == 0 else species_out[...]
+        now = state0[...] if turn == 0 else result[: OWNED * SPEC]
         now = now + coupling * (around - 6.0 * now)
 
         def substep(index, current):
@@ -366,7 +368,7 @@
             return jnp.where(index < counts, current + update, current)
 
         now = lax.fori_loop(0, SUBMAX, substep, now)
-        species_out[...] = now
+        result[: OWNED * SPEC] = now
         theta[turn, 0] = jnp.dot(weights_of[...], now, precision=HIGHEST, preferred_element_type=f32)
 
     def advance_near(cells):
@@ -493,14 +495,16 @@
         arrive(along_z(dz))
         launch(over_square(dz))
     cells = lax.fori_loop(turns // 2, turns, first_turn, cells)
-    send_sums(0).wait_recv()
+    moving = send_sums(0)
+    for dz in range(zn):
+        arrive(over_square(dz))
+        launch(across(dz))
+    moving.wait_recv()
     cchi = scalar_decay(0)
     known[0, 0] = cchi
+    all_known = exchange(lambda j: known.at[0, 0], known, 0, 1, known_send, known_recv)
     for dz in range(zn):
-        arrive(over_square(dz))
-    launch(across())
-    all_known = exchange(lambda j: known.at[0, 0], known, 0, 1, known_send, known_recv)
-    arrive(across())
+        arrive(across(dz))
     advance(0, cchi, cells)
     moving = exchange(lambda j: theta.at[0, 0], theta, 0, 1, theta_send, theta_recv)
     all_known.wait_recv()
@@ -520,7 +524,7 @@
     advance(1, scalar_decay(1), cells)
     exchange(lambda j: theta.at[1, 0], theta, 1, 1, theta_send, theta_recv).wait_recv()
     refine(1)
-    thermal_out[...] = diffuse(1)
+    result[OWNED * SPEC :] = diffuse(1)
 
     for copy in pending:
         copy.wait_send()
@@ -550,14 +554,11 @@
     assert blocks == ndev * OWNED and zs == 128 and rows % (2 * ROWS) == 0
     vmem = pl.BlockSpec(memory_space=pltpu.VMEM)
     dma = pltpu.SemaphoreType.DMA
-    species, thermal = pl.pallas_call(
+    result = pl.pallas_call(
         functools.partial(kernel, gxn, gyn, xs, ys),
-        out_shape=(
-            jax.ShapeDtypeStruct((OWNED * SPEC, ETA), f32),
-            jax.ShapeDtypeStruct((rows, zs), f32),
-        ),
+        out_shape=jax.ShapeDtypeStruct((OWNED * SPEC + rows, zs), f32),
         in_specs=[pl.BlockSpec(memory_space=pltpu.HBM)] * 13,
-        out_specs=(vmem, vmem),
+        out_specs=vmem,
         scratch_shapes=[
             *[pltpu.VMEM((rows, zs), f32)] * 5,
             pltpu.VMEM((rows, zs), i32),
@@ -607,8 +608,8 @@
             dma((1,)),
             dma((STEPS,)),
             dma((STEPS,)),
-            dma((ndev // 2,)),
-            dma((ndev // 2,)),
+            dma((ndev // 2 + gxn,)),
+            dma((ndev // 2 + gxn,)),
             dma((STEPS, 4)),
             dma((STEPS, 4)),
         ],
@@ -630,6 +631,7 @@
         face_partners.T,
         reaction_increments,
     )
+    species, thermal = result[: OWNED * SPEC], result[OWNED * SPEC :]
     return (species.reshape(OWNED, SPEC, ETA), thermal.reshape(xs, ys, zs))
 
 

time: 46.9 us -> 44.1 us (0.940)
  Pallas kernels: 44 us -> 41.8 us
  local copies, waits for them, and re-layouts: 2 us -> 1.4 us
    pallas_call x1, Pallas kernels: 44 us -> 41.8 us  [shards(): pl.pallas_call(functools.partial(kernel, gxn, gyn, xs, ys), out_shape=jax...]
    unnamed x4 -> x0, local copies, waits for them, and re-layouts: 2 us -> none
    slice x0 -> x1, local copies, waits for them, and re-layouts: none -> 1.4 us  [shards(): species, thermal = (result[:OWNED * SPEC], result[OWNED * SPEC:])]
where the time goes in v5:
time: 44.1 us; the launch traced here: 43.9 us
  Pallas kernels  41.8 us (95%)
  local copies, waits for them, and re-layouts  1.4 us (3%)
  between operations  0.64 us (1%)
    pallas_call x1, Pallas kernels, shards(): pl.pallas_call(functools.partial(kernel, gxn, gyn, xs, ys), out_shape=jax...  41.8 us
    slice x1, local copies, waits for them, and re-layouts, shards(): species, thermal = (result[:OWNED * SPEC], result[OWNED * SPEC:])  1.4 us

profile of v5, /device:TPU:0, one launch (start us, length us, event | category | flops | bytes accessed | tf_op | source)
XLA Modules:
  0.0 43.9 jit_solution(13171517854646514663)
XLA Ops:
  0.6 41.8 %shard_map.131 = f32[128,128]{1,0:T(8,128)} custom-call(f32[64,128]{1,0:T(8,128)} %bitcast.12, f32[64,128]{1,0:T(8,128)} %bitcast.13, f32[64,128]{1,0:T(8,128)} %bitcast.14, f32[64,128]{1,0:T(8,128)} %bitcast.15, f32[64,128]{1,0:T(8,128)} %bitcast.16, s32[64,128]{1,0:T(8,128)} %bitcast.17, f32[64,128]{1,0:T(8,128)} %bitcast.18, s32[1,128]{1,0:T(1,128)} %bitcast.22, ...), custom_call_target="tpu_custom_call" | custom-call | tf_op jit(solution)/shard_map/pallas_call | solution.py:557
  42.5 1.4 %fusion = (f32[64,128]{1,0:T(8,128)}, f32[64,128]{1,0:T(8,128)}) fusion(f32[128,128]{1,0:T(8,128)} %shard_map.131), kind=kLoop, calls=%fused_computation | loop fusion | bytes 131072 | tf_op jit(solution)/shard_map/slice | solution.py:634

commit v6 on v5

--- a/solution.py
+++ b/solution.py
@@ -357,13 +357,16 @@
 
         def substep(index, current):
             bent_rows[...] = jnp.tanh(current)
-            sources = [None] * OWNED
+            sources = [None] * (2 * OWNED)
             for t in range(SPEC):
                 column = columns[t]
                 for q in range(OWNED):
                     term = column * bent_rows[q * SPEC + t : q * SPEC + t + 1, :]
-                    sources[q] = term if t == 0 else sources[q] + term
-            source = jnp.concatenate(sources, axis=0)
+                    n = q * 2 + (t & 1)
+                    sources[n] = term if t < 2 else sources[n] + term
+            source = jnp.concatenate(
+                [sources[2 * q] + sources[2 * q + 1] for q in range(OWNED)], axis=0
+            )
             update = mixed * laplacian(current) + reacted * source
             return jnp.where(index < counts, current + update, current)
 

time: 44.1 us -> 44.1 us (level)
  no operation moved by 1% of the time
where the time goes in v6:
time: 44.1 us; the launch traced here: 43.9 us
  Pallas kernels  41.8 us (95%)
  local copies, waits for them, and re-layouts  1.4 us (3%)
  between operations  0.64 us (1%)
    pallas_call x1, Pallas kernels, shards(): pl.pallas_call(functools.partial(kernel, gxn, gyn, xs, ys), out_shape=jax...  41.8 us
    slice x1, local copies, waits for them, and re-layouts, shards(): species, thermal = (result[:OWNED * SPEC], result[OWNED * SPEC:])  1.4 us

profile of v6, /device:TPU:0, one launch (start us, length us, event | category | flops | bytes accessed | tf_op | source)
XLA Modules:
  0.0 43.9 jit_solution(13213059196089470789)
XLA Ops:
  0.6 41.8 %shard_map.131 = f32[128,128]{1,0:T(8,128)} custom-call(f32[64,128]{1,0:T(8,128)} %bitcast.12, f32[64,128]{1,0:T(8,128)} %bitcast.13, f32[64,128]{1,0:T(8,128)} %bitcast.14, f32[64,128]{1,0:T(8,128)} %bitcast.15, f32[64,128]{1,0:T(8,128)} %bitcast.16, s32[64,128]{1,0:T(8,128)} %bitcast.17, f32[64,128]{1,0:T(8,128)} %bitcast.18, s32[1,128]{1,0:T(1,128)} %bitcast.22, ...), custom_call_target="tpu_custom_call" | custom-call | tf_op jit(solution)/shard_map/pallas_call | solution.py:560
  42.5 1.4 %fusion = (f32[64,128]{1,0:T(8,128)}, f32[64,128]{1,0:T(8,128)}) fusion(f32[128,128]{1,0:T(8,128)} %shard_map.131), kind=kLoop, calls=%fused_computation | loop fusion | bytes 131072 | tf_op jit(solution)/shard_map/slice | solution.py:637
